TPU v7x, 1024 devices: a whole 4x4x32 slice. The times are simulated.
1024 devices in a mesh: section: 8 (over z_lo), ctx: 32 (over z_hi, x, core), tp: 4 (over y).
Axes of the slice: x: 4, y: 4, z: 32 (z_hi: 4, z_lo: 8; z = z_hi * 8 + z_lo), core: 2. Of those that a mesh axis runs over, the one named last changes fastest.
Arguments:
- queries: bfloat16 [8, 4096, 8192], P('section', 'ctx', 'tp'), may hold values from -80 to 80
- keys: bfloat16 [8, 4096, 1024], P('section', 'ctx', 'tp'), may hold values from -4 to 4
- values: bfloat16 [8, 4096, 1024], P('section', 'ctx', 'tp'), may hold values from -6 to 6
- span_order: int32 [64], replicated, may hold values from 0 to 63, as said below
Outputs:
- attended: bfloat16 [8, 4096, 8192], P('section', ('ctx', 'tp'))
Inputs may be any that keep to these rules, and one draw needn't show every extreme that they name: `span_order`: a permutation of 0 to 63 in which entries 2 c and 2 c + 1 sum to 63 for every c.
All inputs are finite; a program needn't handle non-finite values.
Results may differ from a plain program's by a relative error of at most 0.0055.
Values may be sent and summed in bfloat16 or wider, within the bound.
No kernel may reach another device: no remote copies, remote signals or barrier semaphores. Data moves between devices by JAX's collectives and lax.ppermute only.
A program may use at most 32 MiB of HBM per device.

v0:
```python
import math

import jax
import jax.numpy as jnp
from jax import lax
from jax.sharding import PartitionSpec as P

HEAD_DIMENSION = 128


def passed_along(array, axis, by):
    peers = lax.axis_size(axis)
    return lax.ppermute(array, axis, [(i, (i + by) % peers) for i in range(peers)])


def sent_together(arrays, axis, dim, along):
    both = jnp.concatenate(arrays, axis=along)
    whole, at, done = (lax.all_gather(both, axis, axis=dim, tiled=True), 0, [])
    for a in arrays:
        done.append(lax.slice_in_dim(whole, at, at + a.shape[along], axis=along))
        at += a.shape[along]
    return tuple(done)


def token_positions(piece_rows, first_row, span_rows, order):
    row_index = first_row + jnp.arange(piece_rows, dtype=jnp.int32)
    span_slot = row_index // span_rows
    matches = span_slot[:, None] == jnp.arange(order.shape[0], dtype=jnp.int32)[None, :]
    span_id = jnp.sum(jnp.where(matches, order[None, :], 0), axis=1)
    return span_id * span_rows + row_index % span_rows


def update(state, query_block, query_pos, key_block, value_block, key_pos, score_scale):
    row_max, row_sum, weighted = state
    scores = (
        jnp.einsum("qkgd,skd->kgqs", query_block, key_block, preferred_element_type=jnp.float32)
        * score_scale
    )
    allowed = key_pos[None, :] <= query_pos[:, None]
    masked = jnp.where(allowed[None, None], scores, jnp.float32(-1e30))
    new_max = jnp.maximum(row_max, jnp.max(masked, axis=-1))
    weights = jnp.where(allowed[None, None], jnp.exp(scores - new_max[..., None]), jnp.float32(0.0))
    rescale = jnp.exp(row_max - new_max)
    row_sum = row_sum * rescale + jnp.sum(weights, axis=-1)
    product = jnp.einsum(
        "kgqs,skd->kgqd",
        weights.astype(jnp.bfloat16),
        value_block,
        preferred_element_type=jnp.float32,
    )
    weighted = weighted * rescale[..., None] + product
    return (new_max, row_sum, weighted)


def shards(queries, keys, values, span_order):
    tokens = queries.shape[1]
    span_rows = tokens // 2
    kv_heads = keys.shape[2] // HEAD_DIMENSION
    query_head_rows = queries.shape[2] // HEAD_DIMENSION
    group_size = query_head_rows // kv_heads
    score_scale = 1.0 / math.sqrt(HEAD_DIMENSION)
    query_pos = token_positions(tokens, lax.axis_index("ctx") * tokens, span_rows, span_order)
    query_pos_parts = query_pos.reshape(2, span_rows)
    one_state = (
        jnp.full((kv_heads, group_size, span_rows), -1e30, jnp.float32),
        jnp.zeros((kv_heads, group_size, span_rows), jnp.float32),
        jnp.zeros((kv_heads, group_size, span_rows, HEAD_DIMENSION), jnp.float32),
    )
    initial = (one_state, one_state)
    received_queries, received_keys, received_values = passed_along(
        (queries, keys, values), "section", 1
    )
    query_parts = received_queries[0].reshape(2, span_rows, kv_heads, group_size, HEAD_DIMENSION)
    key_piece, value_piece = sent_together((received_keys, received_values), "ctx", 1, 0)
    piece_rows = key_piece.shape[1]
    block_count = piece_rows // span_rows
    block_rows = piece_rows // block_count
    key_pos = token_positions(piece_rows, jnp.int32(0), span_rows, span_order).reshape(
        block_count, block_rows
    )
    key_split = key_piece[0].reshape(block_count, block_rows, kv_heads, HEAD_DIMENSION)
    value_split = value_piece[0].reshape(block_count, block_rows, kv_heads, HEAD_DIMENSION)

    def advance(i, current):
        key_block = key_split[i]
        value_block = value_split[i]
        block_pos = key_pos[i]
        updated = []
        for j in range(2):
            updated.append(
                update(
                    current[j],
                    query_parts[j],
                    query_pos_parts[j],
                    key_block,
                    value_block,
                    block_pos,
                    score_scale,
                )
            )
        return tuple(updated)

    states = lax.fori_loop(0, block_count, advance, initial)
    outputs = []
    for j in range(2):
        row_max, row_sum, weighted = states[j]
        result = weighted / row_sum[..., None]
        outputs.append(
            result.transpose(2, 0, 1, 3).reshape(span_rows, query_head_rows * HEAD_DIMENSION)
        )
    attended_local = jnp.concatenate(outputs, axis=0).astype(jnp.bfloat16)[None]
    exchanged = lax.all_to_all(attended_local, "tp", split_axis=1, concat_axis=2, tiled=True)
    return exchanged


def solution(mesh):
    placed = (P("section", "ctx", "tp"), P("section", "ctx", "tp"), P("section", "ctx", "tp"), P())
    return jax.shard_map(
        shards,
        mesh=mesh,
        in_specs=placed,
        out_specs=P("section", ("ctx", "tp"), None),
        check_vma=False,
    )
```

profile of v0, /device:TPU:1, one launch (start us, length us, event | category | flops | bytes accessed | tf_op | source)
XLA Modules:
  0.0 479.7 jit_solution(8877610498605556587)
XLA Ops:
  6.5 4.4 collective-permute-start
  10.9 3.5 collective-permute-start.1
  14.5 7.6 %collective-permute-done = bf16[1,128,256]{2,1,0:T(8,128)(2,1)S(1)} collective-permute-done((bf16[1,128,256]{2,1,0:T(8,128)(2,1)}, bf16[1,128,256]{2,1,0:T(8,128)(2,1)S(1)}, u32[]{:S(2)}, u32[]{:S(2)}) %collective-permute-start) | collective-permute-done | bytes 65568 | tf_op jit(solution)/shard_map/ppermute | solution.py:13
  22.1 1.9 collective-permute-done.1
  24.7 1.9 collective-permute-start.2
  27.4 0.9 select_reduce_fusion.2
  28.6 12.9 %collective-permute-done.2 = bf16[1,128,2048]{2,1,0:T(8,128)(2,1)S(1)} collective-permute-done((bf16[1,128,2048]{2,1,0:T(8,128)(2,1)}, bf16[1,128,2048]{2,1,0:T(8,128)(2,1)S(1)}, u32[]{:S(2)}, u32[]{:S(2)}) %collective-permute-start.2) | collective-permute-done | bytes 524320 | tf_op jit(solution)/shard_map/ppermute | solution.py:13
  41.7 163.6 %all-gather.2.cloned.1.call-done = bf16[2,4096,256]{2,1,0:T(8,128)(2,1)} async-done(((bf16[2,128,256]{2,1,0:T(8,128)(2,1)}), bf16[2,4096,256]{2,1,0:T(8,128)(2,1)}) %all-gather.2.cloned.1.call-update) | async-done | bytes 4194320 | tf_op jit(solution)/shard_map/all_gather | solution.py:18
  205.3 4.5 fusion.32
  209.8 4.0 reshape_squeeze.11
  213.8 4.0 reshape_squeeze.9
  217.8 233.4 %while.24 = (s32[]{:T(128)}, f32[2,8,64]{2,1,0:T(8,128)S(1)}, f32[2,8,64]{2,1,0:T(8,128)S(1)}, f32[2,8,64,128]{3,2,1,0:T(8,128)S(1)}, f32[2,8,64]{2,1,0:T(8,128)...) while((s32[]{:T(128)}, f32[2,8,64]{2,1,0:T(8,128)S(1)}, ...), condition=%wide.region_7.8_spmd.clone, body=%wide.region_2.7_spmd.clone.sunk | while | flops 69093376 | bytes 4630943 | solution.py:103
  221.5 0.8 constant_dynamic-slice_fusion.5
  223.4 0.8 constant_dynamic-slice_fusion.6
  228.8 0.8 constant_dynamic-slice_fusion.5
  232.4 0.8 constant_dynamic-slice_fusion.5
  234.3 0.8 constant_dynamic-slice_fusion.6
  241.6 0.8 constant_dynamic-slice_fusion.6
  245.3 0.8 constant_dynamic-slice_fusion.6
  252.6 0.8 constant_dynamic-slice_fusion.6
  261.6 0.8 constant_dynamic-slice_fusion.5
  263.5 0.8 constant_dynamic-slice_fusion.6
  272.6 0.8 constant_dynamic-slice_fusion.5
  274.5 0.8 constant_dynamic-slice_fusion.6
  279.9 0.8 constant_dynamic-slice_fusion.5
  281.8 0.8 constant_dynamic-slice_fusion.6
  283.5 0.8 constant_dynamic-slice_fusion.5
  290.8 0.8 constant_dynamic-slice_fusion.5
  292.7 0.8 constant_dynamic-slice_fusion.6
  296.4 0.8 constant_dynamic-slice_fusion.6
  301.7 0.8 constant_dynamic-slice_fusion.5
  310.9 0.8 constant_dynamic-slice_fusion.6
  312.7 0.8 constant_dynamic-slice_fusion.5
  320.0 0.8 constant_dynamic-slice_fusion.5
  323.6 0.8 constant_dynamic-slice_fusion.5
  325.5 0.8 constant_dynamic-slice_fusion.6
  329.2 0.8 constant_dynamic-slice_fusion.6
  330.9 0.8 constant_dynamic-slice_fusion.5
  332.8 0.8 constant_dynamic-slice_fusion.6
  340.1 0.8 constant_dynamic-slice_fusion.6
  341.9 0.8 constant_dynamic-slice_fusion.5
  352.8 0.8 constant_dynamic-slice_fusion.5
  360.1 0.8 constant_dynamic-slice_fusion.5
  362.0 0.8 constant_dynamic-slice_fusion.6
  452.2 0.8 copy.60
  453.5 3.7 reduce
  457.6 13.6 %all_to_all.18 = bf16[4,2,32768]{2,1,0:T(2,128)(2,1)S(1)} all-to-all(bf16[4,2,32768]{2,1,0:T(2,128)(2,1)S(1)} %reshape.154), channel_id=1, replica_groups=mesh['section'=8,'ctx'=32,'tp'=4] {'tp'}, dimensions={0} | all-to-all | bytes 1048576 | tf_op jit(solution)/shard_map/all_to_all | solution.py:112
  472.0 0.8 copy.47
  (1022 shorter events, 204.6 us)
Async XLA Ops:
  6.5 198.8 %all-gather.2.cloned.1.call-start = ((), (), s32[]{:S(2)}) async-start(), calls=%async_computation.1 | async-start | bytes 4325376 | tf_op jit(solution)/shard_map/all_gather | solution.py:18
  6.5 15.6 %collective-permute-start = (bf16[1,128,256]{2,1,0:T(8,128)(2,1)}, bf16[1,128,256]{2,1,0:T(8,128)(2,1)S(1)}, u32[]{:S(2)}, u32[]{:S(2)}) collective-permute-start(bf16[1,128,256]{2,1,0:T(8,128)(2,1)} %param.7), channel_id=1, source_target_pairs={{0,128},{128,256},{256,384},{384,512},{512,640},{640,768},{768,896... | collective-permute-start | bytes 196616 | tf_op jit(solution)/shard_map/ppermute | solution.py:13
  10.9 13.1 %collective-permute-start.1 = (bf16[1,128,256]{2,1,0:T(8,128)(2,1)}, bf16[1,128,256]{2,1,0:T(8,128)(2,1)S(1)}, u32[]{:S(2)}, u32[]{:S(2)}) collective-permute-start(bf16[1,128,256]{2,1,0:T(8,128)(2,1)} %param.8), channel_id=1, source_target_pairs={{0,128},{128,256},{256,384},{384,512},{512,640},{640,768},{768,896... | collective-permute-start | bytes 196616 | tf_op jit(solution)/shard_map/ppermute | solution.py:13
  24.7 16.7 %collective-permute-start.2 = (bf16[1,128,2048]{2,1,0:T(8,128)(2,1)}, bf16[1,128,2048]{2,1,0:T(8,128)(2,1)S(1)}, u32[]{:S(2)}, u32[]{:S(2)}) collective-permute-start(bf16[1,128,2048]{2,1,0:T(8,128)(2,1)} %param.6), channel_id=1, source_target_pairs={{0,128},{128,256},{256,384},{384,512},{512,640},{640,768},{768,896... | collective-permute-start | bytes 1572872 | tf_op jit(solution)/shard_map/ppermute | solution.py:13
Sparse Core Ops, SparseCore 0:
  24.8 180.4 all-gather.1
where the time goes:
time: 489 us; the launch traced here: 480 us
  waiting for transfers between devices  186 us (38%)
  local copies, waits for them, and re-layouts  119 us (24%)
  matrix products  100 us (20%)
  other arithmetic  29.3 us (6%)
  blocking collectives  13.6 us (3%)
  between operations  13.6 us (3%)
  starting transfers between devices  9.83 us (2%)
  loops' own time  8.13 us (2%)
    all_gather x1, waiting for transfers between devices, sent_together(): whole, at, done = (lax.all_gather(both, axis, axis=dim, tiled=True), 0, [])  164 us
    dot_general x128, matrix products, update(): jnp.einsum('kgqs,skd->kgqd', weights.astype(jnp.bfloat16), value_block, p...  50.6 us
    dynamic_slice x64, local copies, waits for them, and re-layouts, advance(): value_block = value_split[i]  50.5 us
    dynamic_slice x64, local copies, waits for them, and re-layouts, advance(): key_block = key_split[i]  50.5 us
    dot_general x128, matrix products, update(): jnp.einsum('qkgd,skd->kgqs', query_block, key_block, preferred_element_ty...  49.7 us
    ppermute x3, waiting for transfers between devices, passed_along(): lax.ppermute(array, axis, [(i, (i + by) % peers) for i in range(peers)])  22.4 us
    reduce_sum x128, other arithmetic, update(): row_sum = row_sum * rescale + jnp.sum(weights, axis=-1)  16 us
    all_to_all x1, blocking collectives, shards(): lax.all_to_all(attended_local, 'tp', split_axis=1, concat_axis=2, tiled=T...  13.6 us
  transfers between devices with their start and end apart: 4, of which 4 were waited for; matrix products, arithmetic and copies ran while one was open for 0% of the time, Pallas kernels for 0%

commit v1 on v0

v1 whole, which is shorter than its diff:
```python
import functools
import math

import jax
import jax.numpy as jnp
from jax import lax
from jax.experimental import pallas as pl
from jax.experimental.pallas import tpu as pltpu
from jax.sharding import PartitionSpec as P

HEAD = 128
SPAN = 64
GROUP = 8
SPANS = 64
BLOCK = 256
SCALE = math.log2(math.e) / math.sqrt(HEAD)
LOW = -1e30


def from_section_before(array, swap_cores):
    sections, ring = lax.axis_size("section"), lax.axis_size("ctx")
    pairs = [
        (s * ring + i, ((s + 1) % sections) * ring + (i ^ swap_cores))
        for s in range(sections)
        for i in range(ring)
    ]
    return lax.ppermute(array, ("section", "ctx"), pairs)


def along_x(array, by):
    pairs = [(i, (i // 8) * 8 + ((i % 8 // 2 + by) % 4) * 2 + i % 2) for i in range(32)]
    return lax.ppermute(array, "ctx", pairs)


def kernel(sources, first, last, order, own, other, *rest):
    rest = list(rest)
    chunks = [rest.pop(0) for _ in sources]
    if not first:
        acc_in, top_in, total_in = [rest.pop(0) for _ in range(3)]
    if last:
        out = rest.pop(0)
    acc, top, total = [rest.pop(0) for _ in range(3)]
    q_rows, k_sorted, v_sorted, held_by, row_of, place_of, counts = rest
    ctx = lax.axis_index("ctx")
    my_x, my_core = (ctx % 8) // 2, ctx % 2

    def place(i, carry):
        held_by[order[i]] = i
        return carry

    lax.fori_loop(0, SPANS, place, 0, unroll=8)

    def sort(p, filled):
        i = held_by[p]
        owner = i // 2
        source = (my_x - (owner % 8) // 2 + 4) % 4
        row = (owner // 8) * 256 + ((owner + my_core) % 2) * 128 + (i % 2) * SPAN
        updated = []
        for at, d in enumerate(sources):
            row_of[at, filled[at]] = row
            place_of[at, filled[at]] = p
            updated.append(filled[at] + (source == d).astype(jnp.int32))
            counts[at, p] = updated[at]
        return tuple(updated)

    lax.fori_loop(0, SPANS, sort, (jnp.int32(0),) * len(sources), unroll=4)

    places = []
    for j, ref in enumerate((own, other)):
        owner = ctx if j == 0 else ctx + 1 - 2 * my_core
        for e in range(2):
            places.append(order[2 * owner + e])
            for h in range(GROUP):
                q_rows[2 * j + e, h * SPAN : (h + 1) * SPAN, :] = ref[
                    e * SPAN : (e + 1) * SPAN, 2 * HEAD + h * HEAD : 2 * HEAD + (h + 1) * HEAD
                ]

    if first:
        acc[...] = jnp.zeros_like(acc)
        top[...] = jnp.full_like(top, LOW)
        total[...] = jnp.zeros_like(total)
    else:
        acc[...] = acc_in[...]
        top[...] = top_in[...]
        total[...] = total_in[...]

    width = GROUP * SPAN
    if 0 in sources:
        key_row = lax.broadcasted_iota(jnp.int32, (SPAN, width), 0)
        query_row = lax.broadcasted_iota(jnp.int32, (SPAN, width), 1) % SPAN
        later_by = key_row - query_row

    for at, (d, chunk) in enumerate(zip(sources, chunks)):
        for two in range(8):
            rows = [
                chunk[pl.ds(pl.multiple_of(row_of[at, 2 * two + u], SPAN), SPAN), :]
                for u in range(2)
            ]
            both = jnp.concatenate(rows, axis=0)
            k_sorted[at, two * 128 : (two + 1) * 128, :] = both[:, :HEAD]
            v_sorted[at, :, two * 128 : (two + 1) * 128] = both[:, HEAD:].T
        for j in range(2):
            low_spans = counts[at, places[2 * j]]
            high_spans = counts[at, places[2 * j + 1]]
            low_blocks = (low_spans + 3) // 4
            used, highs, valid, scores, starts = [], [], [], [], []
            for t in range(5):
                high = t >= low_blocks
                b = jnp.minimum(jnp.where(high, t - low_blocks, t), 3)
                spans = jnp.where(high, high_spans, low_spans)
                start = pl.multiple_of(b * BLOCK, BLOCK)
                s = 2 * j + high.astype(jnp.int32)
                block = lax.dot_general(
                    k_sorted[at, pl.ds(start, BLOCK), :],
                    q_rows[s],
                    (((1,), (1,)), ((), ())),
                    preferred_element_type=jnp.float32,
                )
                fresh = jnp.logical_or(jnp.logical_not(high), t - low_blocks < 4)
                for u in range(4):
                    part = block[u * SPAN : (u + 1) * SPAN]
                    if d == 0:
                        key_place = place_of[at, b * 4 + u]
                        slack = (jnp.where(high, places[2 * j + 1], places[2 * j]) - key_place) * SPAN
                        part = jnp.where(later_by <= slack, part, LOW)
                    scores.append(part.reshape(SPAN // 8, 8, width))
                    valid.append(jnp.logical_and(fresh, b * 4 + u < spans))
                    highs.append(high)
                used.append(s)
                starts.append(start)
            peaks = [jnp.max(part, axis=0) for part in scores]
            now, fade = [], []
            for e in range(2):
                peak = jnp.full((8, width), LOW, jnp.float32)
                for part, ok, high in zip(peaks, valid, highs):
                    ours = high if e else jnp.logical_not(high)
                    peak = jnp.maximum(peak, jnp.where(jnp.logical_and(ok, ours), part, LOW))
                peak = jnp.max(peak, axis=0, keepdims=True)
                before = top[2 * j + e]
                new = jnp.maximum(before, jnp.broadcast_to(peak, (8, width)))
                top[2 * j + e] = new
                now.append(new * SCALE)
                fade.append(jnp.exp2((before - new) * SCALE))
            for e in range(2):
                s = 2 * j + e
                acc[s] = (acc[s].reshape(HEAD // 8, 8, width) * fade[e][None]).reshape(HEAD, width)
                total[s] = total[s] * fade[e]
            for t in range(5):
                weights, added = [], jnp.zeros((8, width), jnp.float32)
                for u in range(4):
                    i = 4 * t + u
                    base = jnp.where(valid[i], jnp.where(highs[i], now[1], now[0]), -LOW)
                    w = jnp.exp2(scores[i] * SCALE - base[None])
                    added = added + jnp.sum(w, axis=0)
                    weights.append(w.reshape(SPAN, width).astype(jnp.bfloat16))
                total[used[t]] = total[used[t]] + added
                acc[used[t]] = acc[used[t]] + jnp.dot(
                    v_sorted[at, :, pl.ds(starts[t], BLOCK)],
                    jnp.concatenate(weights, axis=0),
                    preferred_element_type=jnp.float32,
                )

    if last:
        for j in range(2):
            core = my_core if j == 0 else 1 - my_core
            for e in range(2):
                s = 2 * j + e
                result = (acc[s] / jnp.sum(total[s], axis=0, keepdims=True)).T.astype(jnp.bfloat16)
                for f in range(2):
                    for h in range(GROUP):
                        at = h * SPAN + f * 32
                        out[core, 2 * e + f, :, h * HEAD : (h + 1) * HEAD] = result[at : at + 32]


def attend(order, own, other, chunks, sources, state=None, last=True):
    first = state is None
    state_shapes = (
        jax.ShapeDtypeStruct((4, HEAD, GROUP * SPAN), jnp.float32),
        jax.ShapeDtypeStruct((4, 8, GROUP * SPAN), jnp.float32),
        jax.ShapeDtypeStruct((4, 8, GROUP * SPAN), jnp.float32),
    )
    own_state = [pltpu.VMEM(s.shape, s.dtype) for s in state_shapes] if last else []
    n = len(chunks)
    scratch = own_state + [
        pltpu.VMEM((4, GROUP * SPAN, HEAD), jnp.bfloat16),
        pltpu.VMEM((n, 1024, HEAD), jnp.bfloat16),
        pltpu.VMEM((n, HEAD, 1024), jnp.bfloat16),
        pltpu.SMEM((SPANS,), jnp.int32),
        pltpu.SMEM((n, 17), jnp.int32),
        pltpu.SMEM((n, 17), jnp.int32),
        pltpu.SMEM((n, SPANS), jnp.int32),
    ]
    vmem = pl.BlockSpec(memory_space=pltpu.VMEM)
    inputs = [own, other, *chunks, *([] if first else state)]
    output = jax.ShapeDtypeStruct((2, 4, 32, GROUP * HEAD), jnp.bfloat16)
    pairs = n * 2 * 20 * SPAN * GROUP * SPAN
    return pl.pallas_call(
        functools.partial(kernel, tuple(sources), first, last),
        out_shape=output if last else state_shapes,
        in_specs=[pl.BlockSpec(memory_space=pltpu.SMEM)] + [vmem] * len(inputs),
        out_specs=vmem if last else (vmem,) * 3,
        scratch_shapes=scratch,
        compiler_params=pltpu.CompilerParams(vmem_limit_bytes=40 * 1024 * 1024),
        cost_estimate=pl.CostEstimate(
            flops=4 * pairs * HEAD, bytes_accessed=4 * 1024 * 1024, transcendentals=pairs
        ),
    )(order, *inputs)


def shards(queries, keys, values, span_order):
    core = lax.axis_index("ctx") % 2
    half = GROUP * HEAD
    heads = [
        jnp.concatenate(
            [a[0][:, h * HEAD : (h + 1) * HEAD] for a in (keys, values)]
            + [queries[0][:, h * half : (h + 1) * half]],
            axis=1,
        )
        for h in range(2)
    ]
    own, other = jnp.where(core == 0, heads[0], heads[1]), jnp.where(core == 0, heads[1], heads[0])
    own, other = from_section_before(own, 0), from_section_before(other, 1)
    chip_kv = jnp.concatenate([own[:, : 2 * HEAD], other[:, : 2 * HEAD]], axis=0)
    planes = [[z * 8 + r for z in range(4)] for r in range(8)]
    column = lax.all_gather(chip_kv, "ctx", axis=0, tiled=True, axis_index_groups=planes)
    chunks = {d: along_x(column, d) for d in (1, 3, 2)}
    state = attend(span_order, own, other, [column], (0,), last=False)
    state = attend(span_order, own, other, [chunks[1]], (1,), state, last=False)
    state = attend(span_order, own, other, [chunks[3]], (3,), state, last=False)
    out = attend(span_order, own, other, [chunks[2]], (2,), state)
    out = out.reshape(8, 32, half)
    peers = [[(chip * 2 + c) * 4 + y for c in range(2) for y in range(4)] for chip in range(16)]
    out = lax.all_to_all(
        out, ("ctx", "tp"), split_axis=0, concat_axis=0, tiled=True, axis_index_groups=peers
    )
    out = out.reshape(2, 4, 32, half).transpose(2, 1, 0, 3)
    return out.reshape(1, 32, 8 * half)


def solution(mesh):
    placed = (P("section", "ctx", "tp"), P("section", "ctx", "tp"), P("section", "ctx", "tp"), P())
    return jax.shard_map(
        shards,
        mesh=mesh,
        in_specs=placed,
        out_specs=P("section", ("ctx", "tp"), None),
        check_vma=False,
    )
```

time: 489 us -> 144 us (0.29); the launches traced: 480 us -> 144 us
  waiting for transfers between devices: 186 us -> 29.6 us
  local copies, waits for them, and re-layouts: 119 us -> 2.88 us
  matrix products: 100 us -> 0 us
  blocking collectives: 13.6 us -> 72.1 us
  other arithmetic: 29.3 us -> 0.12 us
  Pallas kernels: 0 us -> 20.2 us
  between operations: 13.6 us -> 0.14 us
  starting transfers between devices: 9.83 us -> 18.7 us
  loops' own time: 8.13 us -> 0 us
    all_gather x1 -> x0, waiting for transfers between devices: 164 us -> none  [sent_together(): whole, at, done = (lax.all_gather(both, axis, axis=dim, tiled=True), 0, [])]
    dynamic_slice x192 -> x0, local copies, waits for them, and re-layouts: 102 us -> none  [the longest x64 50.5 us: advance(): value_block = value_split[i]]
    dot_general x256 -> x0, matrix products: 100 us -> none  [the longest x128 50.6 us: update(): jnp.einsum('kgqs,skd->kgqd', weights.astype(jnp.bfloat16), value_block, p...]
    all_gather x0 -> x1, blocking collectives: none -> 50.9 us  [shards(): lax.all_gather(chip_kv, 'ctx', axis=0, tiled=True, axis_index_groups=planes)]
    pallas_call x0 -> x4, Pallas kernels: none -> 20.2 us  [attend(): pl.pallas_call(functools.partial(kernel, tuple(sources), first, last), ou...]
    reduce_sum x130 -> x0, other arithmetic: 17.6 us -> none  [the longest x128 16 us: update(): row_sum = row_sum * rescale + jnp.sum(weights, axis=-1)]
    ppermute x3 -> x5, starting transfers between devices: 9.83 us -> 18.7 us  [the longest x3 9.92 us: along_x(): return lax.ppermute(array, 'ctx', pairs)]
    another operation x1 -> x0, loops' own time: 8.13 us -> none  [shards(): states = lax.fori_loop(0, block_count, advance, initial)]
  transfers between devices with their start and end apart: 4 -> 5, of which waited for: 4 -> 4; matrix products, arithmetic and copies ran while one was open for 0% -> 0% of each run, Pallas kernels for 0% -> 10%
where the time goes in v1:
time: 144 us
  blocking collectives  72.1 us (50%)
  waiting for transfers between devices  29.6 us (21%)
  Pallas kernels  20.2 us (14%)
  starting transfers between devices  18.7 us (13%)
  local copies, waits for them, and re-layouts  2.88 us (2%)
    all_gather x1, blocking collectives, shards(): lax.all_gather(chip_kv, 'ctx', axis=0, tiled=True, axis_index_groups=planes)  50.9 us
    ppermute x2, waiting for transfers between devices, from_section_before(): return lax.ppermute(array, ('section', 'ctx'), pairs)  27.3 us
    all_to_all x1, blocking collectives, shards(): lax.all_to_all(out, ('ctx', 'tp'), split_axis=0, concat_axis=0, tiled=Tru...  21.2 us
    pallas_call x4, Pallas kernels, attend(): pl.pallas_call(functools.partial(kernel, tuple(sources), first, last), ou...  20.2 us
    ppermute x3, starting transfers between devices, along_x(): return lax.ppermute(array, 'ctx', pairs)  9.92 us
    ppermute x2, starting transfers between devices, from_section_before(): return lax.ppermute(array, ('section', 'ctx'), pairs)  8.76 us
  transfers between devices with their start and end apart: 5, of which 4 were waited for; matrix products, arithmetic and copies ran while one was open for 0% of the time, Pallas kernels for 10%

profile of v1, /device:TPU:1, one launch (start us, length us, event | category | flops | bytes accessed | tf_op | source)
XLA Modules:
  0.0 143.8 jit_solution(8440004783481277259)
XLA Ops:
  0.0 0.0 copy-start.1
  0.0 0.0 copy-start.2
  0.0 1.1 fusion
  1.1 0.0 copy-done.1
  1.1 0.0 copy-done.2
  1.2 0.1 broadcast_select_fusion
  1.3 4.4 %collective-permute-start = (bf16[128,1280]{1,0:T(8,128)(2,1)S(1)}, bf16[128,1280]{1,0:T(8,128)(2,1)S(1)}, u32[]{:S(2)}, u32[]{:S(2)}) collective-permute-start(bf16[128,1280]{1,0:T(8,128)(2,1)S(1)} %get-tuple-element.24), channel_id=1, source_target_pairs={{0,128},{4,132},{8,136},{12,140},{16,144},{20,148},{24,152},{28,15... | collective-permute-start | bytes 983048 | tf_op jit(solution)/shard_map/ppermute | solution.py:27
  5.7 4.4 %collective-permute-start.1 = (bf16[128,1280]{1,0:T(8,128)(2,1)S(1)}, bf16[128,1280]{1,0:T(8,128)(2,1)S(1)}, u32[]{:S(2)}, u32[]{:S(2)}) collective-permute-start(bf16[128,1280]{1,0:T(8,128)(2,1)S(1)} %get-tuple-element.23), channel_id=1, source_target_pairs={{0,132},{4,128},{8,140},{12,136},{16,148},{20,144},{24,156},{28,15... | collective-permute-start | bytes 983048 | tf_op jit(solution)/shard_map/ppermute | solution.py:27
  10.1 9.4 %collective-permute-done.own = bf16[128,1280]{1,0:T(8,128)(2,1)S(1)} collective-permute-done((bf16[128,1280]{1,0:T(8,128)(2,1)S(1)}, bf16[128,1280]{1,0:T(8,128)(2,1)S(1)}, u32[]{:S(2)}, u32[]{:S(2)}) %collective-permute-start) | collective-permute-done | bytes 327712 | tf_op jit(solution)/shard_map/ppermute | solution.py:27
  19.5 17.9 %collective-permute-done.1.other = bf16[128,1280]{1,0:T(8,128)(2,1)S(1)} collective-permute-done((bf16[128,1280]{1,0:T(8,128)(2,1)S(1)}, bf16[128,1280]{1,0:T(8,128)(2,1)S(1)}, u32[]{:S(2)}, u32[]{:S(2)}) %collective-permute-start.1) | collective-permute-done | bytes 327712 | tf_op jit(solution)/shard_map/ppermute | solution.py:27
  37.4 0.0 copy-start
  37.4 50.9 %all_gather.3.rest_0_ = bf16[1024,256]{1,0:T(8,128)(2,1)S(1)} all-gather(bf16[256,256]{1,0:T(8,128)(2,1)S(1)} %pad_maximum_fusion.2), channel_id=1, replica_groups={{0,32,64,96},{4,36,68,100},{8,40,72,104},{12,44,76,108},{16,48,80,112},..., dimensions={0}, use_global_device_ids=true | all-gather | bytes 655360 | tf_op jit(solution)/shard_map/all_gather | solution.py:225
  88.3 3.1 %collective-permute-start.4 = (bf16[1024,256]{1,0:T(8,128)(2,1)S(1)}, bf16[1024,256]{1,0:T(8,128)(2,1)S(1)}, u32[]{:S(2)}, u32[]{:S(2)}) collective-permute-start(bf16[1024,256]{1,0:T(8,128)(2,1)S(1)} %all_gather.3.rest_0_), channel_id=1, source_target_pairs={{0,8},{4,12},{8,16},{12,20},{16,24},{20,28},{24,0},{28,4},{32,40},... | collective-permute-start | bytes 1572872 | tf_op jit(solution)/shard_map/ppermute | solution.py:32
  91.4 3.4 %collective-permute-start.3 = (bf16[1024,256]{1,0:T(8,128)(2,1)S(1)}, bf16[1024,256]{1,0:T(8,128)(2,1)S(1)}, u32[]{:S(2)}, u32[]{:S(2)}) collective-permute-start(bf16[1024,256]{1,0:T(8,128)(2,1)S(1)} %all_gather.3.rest_0_), channel_id=1, source_target_pairs={{0,24},{4,28},{8,0},{12,4},{16,8},{20,12},{24,16},{28,20},{32,56},... | collective-permute-start | bytes 1572872 | tf_op jit(solution)/shard_map/ppermute | solution.py:32
  94.8 3.4 %collective-permute-start.2 = (bf16[1024,256]{1,0:T(8,128)(2,1)S(1)}, bf16[1024,256]{1,0:T(8,128)(2,1)S(1)}, u32[]{:S(2)}, u32[]{:S(2)}) collective-permute-start(bf16[1024,256]{1,0:T(8,128)(2,1)S(1)} %all_gather.3.rest_0_), channel_id=1, source_target_pairs={{0,16},{4,20},{8,24},{12,28},{16,0},{20,4},{24,8},{28,12},{32,48},... | collective-permute-start | bytes 1572872 | tf_op jit(solution)/shard_map/ppermute | solution.py:32
  98.2 0.0 copy-done
  98.2 5.0 %shard_map.46 = (f32[4,128,512]{2,1,0:T(8,128)S(1)}, f32[4,8,512]{2,1,0:T(8,128)S(1)}, f32[4,8,512]{2,1,0:T(8,128)S(1)}) custom-call(s32[64]{0:T(128)S(1)} %copy-done, bf16[128,1280]{1,0:T(8,128)(2,1)S(1)} %collective-permute-done.own, bf16[128,1280]{1,0:T(8,128)(2,1)S(1)} %collective-permute-done.1.other, bf16[1024,256]{1,0:T(8,128)(2,1)S(1)} %all_gather.3.rest_0_), custom_call_target="tpu_custom_call" | custom-call | flops 671088640 | bytes 4194304 | tf_op jit(solution)/shard_map/pallas_call | solution.py:197
  103.2 0.1 collective-permute-done.4.rest_0_
  103.4 5.0 %shard_map.47 = (f32[4,128,512]{2,1,0:T(8,128)S(1)}, f32[4,8,512]{2,1,0:T(8,128)S(1)}, f32[4,8,512]{2,1,0:T(8,128)S(1)}) custom-call(s32[64]{0:T(128)S(1)} %copy-done, bf16[128,1280]{1,0:T(8,128)(2,1)S(1)} %collective-permute-done.own, bf16[128,1280]{1,0:T(8,128)(2,1)S(1)} %collective-permute-done.1.other, ...), custom_call_target="tpu_custom_call" | custom-call | flops 671088640 | bytes 4194304 | tf_op jit(solution)/shard_map/pallas_call | solution.py:197
  108.4 0.0 collective-permute-done.3.rest_0_
  108.4 5.0 %shard_map.48 = (f32[4,128,512]{2,1,0:T(8,128)S(1)}, f32[4,8,512]{2,1,0:T(8,128)S(1)}, f32[4,8,512]{2,1,0:T(8,128)S(1)}) custom-call(s32[64]{0:T(128)S(1)} %copy-done, bf16[128,1280]{1,0:T(8,128)(2,1)S(1)} %collective-permute-done.own, bf16[128,1280]{1,0:T(8,128)(2,1)S(1)} %collective-permute-done.1.other, ...), custom_call_target="tpu_custom_call" | custom-call | flops 671088640 | bytes 4194304 | tf_op jit(solution)/shard_map/pallas_call | solution.py:197
  113.4 2.2 %collective-permute-done.2.rest_0_ = bf16[1024,256]{1,0:T(8,128)(2,1)S(1)} collective-permute-done((bf16[1024,256]{1,0:T(8,128)(2,1)S(1)}, bf16[1024,256]{1,0:T(8,128)(2,1)S(1)}, u32[]{:S(2)}, u32[]{:S(2)}) %collective-permute-start.2) | collective-permute-done | bytes 524320 | tf_op jit(solution)/shard_map/ppermute | solution.py:32
  115.6 5.2 %shard_map.49 = bf16[2,4,32,1024]{3,2,1,0:T(8,128)(2,1)S(1)} custom-call(s32[64]{0:T(128)S(1)} %copy-done, bf16[128,1280]{1,0:T(8,128)(2,1)S(1)} %collective-permute-done.own, bf16[128,1280]{1,0:T(8,128)(2,1)S(1)} %collective-permute-done.1.other, bf16[1024,256]{1,0:T(8,128)(2,1)S(1)} %collective-permute-done.2.rest_0_, ...), custom_call_target="tpu_custom_call" | custom-call | flops 671088640 | bytes 4194304 | tf_op jit(solution)/shard_map/pallas_call | solution.py:197
  120.8 21.2 %all_to_all.5 = bf16[8,32,1024]{2,1,0:T(8,128)(2,1)S(1)} all-to-all(bf16[8,32,1024]{2,1,0:T(8,128)(2,1)S(1)} %bitcast.8), channel_id=1, replica_groups={{0,1,2,3,4,5,6,7},{8,9,10,11,12,13,14,15},{16,17,18,19,20,21,22,23},{24..., dimensions={0} | all-to-all | bytes 1048576 | tf_op jit(solution)/shard_map/all_to_all | solution.py:233
  142.0 0.5 copy.7
  142.6 1.2 reshape.11
  (4 shorter events, 0.0 us)
Async XLA Ops:
  0.0 1.1 copy-start.1
  0.0 1.1 copy-start.2
  1.3 18.2 %collective-permute-start = (bf16[128,1280]{1,0:T(8,128)(2,1)S(1)}, bf16[128,1280]{1,0:T(8,128)(2,1)S(1)}, u32[]{:S(2)}, u32[]{:S(2)}) collective-permute-start(bf16[128,1280]{1,0:T(8,128)(2,1)S(1)} %get-tuple-element.24), channel_id=1, source_target_pairs={{0,128},{4,132},{8,136},{12,140},{16,144},{20,148},{24,152},{28,15... | collective-permute-start | bytes 983048 | tf_op jit(solution)/shard_map/ppermute | solution.py:27
  5.7 31.7 %collective-permute-start.1 = (bf16[128,1280]{1,0:T(8,128)(2,1)S(1)}, bf16[128,1280]{1,0:T(8,128)(2,1)S(1)}, u32[]{:S(2)}, u32[]{:S(2)}) collective-permute-start(bf16[128,1280]{1,0:T(8,128)(2,1)S(1)} %get-tuple-element.23), channel_id=1, source_target_pairs={{0,132},{4,128},{8,140},{12,136},{16,148},{20,144},{24,156},{28,15... | collective-permute-start | bytes 983048 | tf_op jit(solution)/shard_map/ppermute | solution.py:27
  37.4 60.8 %copy-start = (s32[64]{0:T(128)S(1)}, s32[64]{0:T(128)}, u32[]{:S(2)}) copy-start(s32[64]{0:T(128)} %order.7) | copy-start | bytes 772
  88.3 15.1 %collective-permute-start.4 = (bf16[1024,256]{1,0:T(8,128)(2,1)S(1)}, bf16[1024,256]{1,0:T(8,128)(2,1)S(1)}, u32[]{:S(2)}, u32[]{:S(2)}) collective-permute-start(bf16[1024,256]{1,0:T(8,128)(2,1)S(1)} %all_gather.3.rest_0_), channel_id=1, source_target_pairs={{0,8},{4,12},{8,16},{12,20},{16,24},{20,28},{24,0},{28,4},{32,40},... | collective-permute-start | bytes 1572872 | tf_op jit(solution)/shard_map/ppermute | solution.py:32
  91.4 17.0 %collective-permute-start.3 = (bf16[1024,256]{1,0:T(8,128)(2,1)S(1)}, bf16[1024,256]{1,0:T(8,128)(2,1)S(1)}, u32[]{:S(2)}, u32[]{:S(2)}) collective-permute-start(bf16[1024,256]{1,0:T(8,128)(2,1)S(1)} %all_gather.3.rest_0_), channel_id=1, source_target_pairs={{0,24},{4,28},{8,0},{12,4},{16,8},{20,12},{24,16},{28,20},{32,56},... | collective-permute-start | bytes 1572872 | tf_op jit(solution)/shard_map/ppermute | solution.py:32
  94.8 20.8 %collective-permute-start.2 = (bf16[1024,256]{1,0:T(8,128)(2,1)S(1)}, bf16[1024,256]{1,0:T(8,128)(2,1)S(1)}, u32[]{:S(2)}, u32[]{:S(2)}) collective-permute-start(bf16[1024,256]{1,0:T(8,128)(2,1)S(1)} %all_gather.3.rest_0_), channel_id=1, source_target_pairs={{0,16},{4,20},{8,24},{12,28},{16,0},{20,4},{24,8},{28,12},{32,48},... | collective-permute-start | bytes 1572872 | tf_op jit(solution)/shard_map/ppermute | solution.py:32

commit v2 on v1

v2 whole, which is shorter than its diff:
```python
import functools
import math

import jax
import jax.numpy as jnp
from jax import lax
from jax.experimental import pallas as pl
from jax.experimental.pallas import tpu as pltpu
from jax.sharding import PartitionSpec as P

HEAD = 128
SPAN = 64
GROUP = 8
SPANS = 64
BLOCK = 256
SCALE = math.log2(math.e) / math.sqrt(HEAD)
LOW = -1e30
DIRECT = 384
PLACE, COUNT, MINE = 17, 34, 38


def between_cores(array):
    return lax.ppermute(array, "ctx", [(i, i ^ 1) for i in range(lax.axis_size("ctx"))])


def to_next_section(array, along_y):
    sections, peers = lax.axis_size("section"), lax.axis_size("tp")
    pairs = [
        (s * peers + y, ((s + 1) % sections) * peers + (y + along_y) % peers)
        for s in range(sections)
        for y in range(peers)
    ]
    return lax.ppermute(array, ("section", "tp"), pairs)


def along_x(array, by):
    pairs = [(i, (i // 8) * 8 + ((i % 8 // 2 + by) % 4) * 2 + i % 2) for i in range(32)]
    return lax.ppermute(array, "ctx", pairs)


def make_plan(order, plan, held_by, counts):
    ctx = lax.axis_index("ctx")
    my_x, my_core = (ctx >> 1) & 3, ctx & 1

    def place(i, carry):
        held_by[order[i]] = i
        return carry

    lax.fori_loop(0, SPANS, place, 0, unroll=8)

    def sort(p, filled):
        i = held_by[p]
        source = (my_x - (i >> 2)) & 3
        row = ((i >> 4) << 8) | ((((i >> 1) ^ my_core) & 1) << 7) | ((i & 1) << 6)
        updated = []
        for d in range(4):
            plan[d, filled[d]] = row
            plan[d, PLACE + filled[d]] = p
            updated.append(filled[d] + (source == d).astype(jnp.int32))
            counts[d, p] = updated[d]
        return tuple(updated)

    lax.fori_loop(0, SPANS, sort, (jnp.int32(0),) * 4, unroll=4)
    for j in range(2):
        owner = ctx if j == 0 else ctx + 1 - 2 * my_core
        for e in range(2):
            place = order[2 * owner + e]
            for d in range(4):
                plan[d, COUNT + 2 * j + e] = counts[d, place]
                plan[d, MINE + 2 * j + e] = place


def kernel(sources, groups, first, last, *refs):
    refs = list(refs)
    given, own, other = [refs.pop(0) for _ in range(3)]
    chunks = [[refs.pop(0) for _ in range(pieces)] for _, pieces in sources]
    if not first:
        acc_in, top_in, total_in = [refs.pop(0) for _ in range(3)]
    if last:
        out = refs.pop(0)
    acc, top, total = [refs.pop(0) for _ in range(3)]
    plan = refs.pop(0) if first else given
    q_rows, k_sorted, v_sorted = [refs.pop(0) for _ in range(3)]
    if first:
        make_plan(given, plan, *refs)
    places = [plan[0, MINE + s] for s in range(4)]
    for j in groups:
        ref = (own, other)[j]
        for e in range(2):
            for h in range(GROUP):
                q_rows[2 * j + e, h * SPAN : (h + 1) * SPAN, :] = ref[
                    e * SPAN : (e + 1) * SPAN, h * HEAD : (h + 1) * HEAD
                ]

    if first:
        acc[...] = jnp.zeros_like(acc)
        top[...] = jnp.full_like(top, LOW)
        total[...] = jnp.zeros_like(total)
    else:
        for j in groups:
            for ref, given in ((acc, acc_in), (top, top_in), (total, total_in)):
                ref[2 * j : 2 * j + 2] = given[2 * j : 2 * j + 2]

    width = GROUP * SPAN
    if first:
        key_row = lax.broadcasted_iota(jnp.int32, (SPAN, width), 0)
        query_row = lax.broadcasted_iota(jnp.int32, (SPAN, width), 1) % SPAN
        later_by = key_row - query_row

    for (source, pieces), chunk in zip(sources, chunks):
        if pieces == 1:
            chunk = chunk[0]
        else:
            whole, at = refs[0], 0
            for piece in chunk:
                whole[at : at + piece.shape[0], :] = piece[...]
                at += piece.shape[0]
            chunk = whole
        for two in range(8):
            rows = [
                chunk[pl.ds(pl.multiple_of(plan[source, 2 * two + u], SPAN), SPAN), :]
                for u in range(2)
            ]
            both = jnp.concatenate(rows, axis=0)
            k_sorted[two * 128 : (two + 1) * 128, :] = both[:, :HEAD]
            v_sorted[:, two * 128 : (two + 1) * 128] = both[:, HEAD:].T
        for j in groups:
            low_spans = plan[source, COUNT + 2 * j]
            high_spans = plan[source, COUNT + 2 * j + 1]
            low_blocks = (low_spans + 3) // 4
            used, highs, valid, scores, starts = [], [], [], [], []
            for t in range(5):
                high = t >= low_blocks
                b = jnp.minimum(jnp.where(high, t - low_blocks, t), 3)
                spans = jnp.where(high, high_spans, low_spans)
                start = pl.multiple_of(b * BLOCK, BLOCK)
                s = 2 * j + high.astype(jnp.int32)
                block = lax.dot_general(
                    k_sorted[pl.ds(start, BLOCK), :],
                    q_rows[s],
                    (((1,), (1,)), ((), ())),
                    preferred_element_type=jnp.float32,
                )
                fresh = jnp.logical_or(jnp.logical_not(high), t - low_blocks < 4)
                for u in range(4):
                    part = block[u * SPAN : (u + 1) * SPAN]
                    if first:
                        key_place = plan[source, PLACE + b * 4 + u]
                        mine = jnp.where(high, places[2 * j + 1], places[2 * j])
                        slack = (mine - key_place) * SPAN
                        part = jnp.where(later_by <= slack, part, LOW)
                    scores.append(part.reshape(SPAN // 8, 8, width))
                    valid.append(jnp.logical_and(fresh, b * 4 + u < spans))
                    highs.append(high)
                used.append(s)
                starts.append(start)
            peaks = [jnp.max(part, axis=0) for part in scores]
            now, fade = [], []
            for e in range(2):
                peak = jnp.full((8, width), LOW, jnp.float32)
                for part, ok, high in zip(peaks, valid, highs):
                    ours = high if e else jnp.logical_not(high)
                    peak = jnp.maximum(peak, jnp.where(jnp.logical_and(ok, ours), part, LOW))
                peak = jnp.max(peak, axis=0, keepdims=True)
                before = top[2 * j + e]
                new = jnp.maximum(before, jnp.broadcast_to(peak, (8, width)))
                top[2 * j + e] = new
                now.append(new * SCALE)
                fade.append(jnp.exp2((before - new) * SCALE))
            for e in range(2):
                s = 2 * j + e
                acc[s] = (acc[s].reshape(HEAD // 8, 8, width) * fade[e][None]).reshape(HEAD, width)
                total[s] = total[s] * fade[e]
            for t in range(5):
                weights, added = [], jnp.zeros((8, width), jnp.float32)
                for u in range(4):
                    i = 4 * t + u
                    base = jnp.where(valid[i], jnp.where(highs[i], now[1], now[0]), -LOW)
                    w = jnp.exp2(scores[i] * SCALE - base[None])
                    added = added + jnp.sum(w, axis=0)
                    weights.append(w.reshape(SPAN, width).astype(jnp.bfloat16))
                total[used[t]] = total[used[t]] + added
                acc[used[t]] = acc[used[t]] + jnp.dot(
                    v_sorted[:, pl.ds(starts[t], BLOCK)],
                    jnp.concatenate(weights, axis=0),
                    preferred_element_type=jnp.float32,
                )

    if last:
        my_y = lax.axis_index("tp")
        (j,) = groups
        for e in range(2):
            inverse = 1.0 / jnp.sum(total[2 * j + e], axis=0, keepdims=True)
            result = (acc[2 * j + e] * inverse).T.astype(jnp.bfloat16)
            for f in range(2):
                for h in range(GROUP):
                    at = h * SPAN + f * 32
                    out[(2 * e + f - my_y) & 3, :, h * HEAD : (h + 1) * HEAD] = result[at : at + 32]


def join(*refs):
    *pieces, out = refs
    for d, piece in enumerate(pieces):
        at = pl.multiple_of(((lax.axis_index("tp") - d) & 3) * piece.shape[1], HEAD)
        out[:, pl.ds(at, piece.shape[1])] = piece[...]


def attend(plan, own, other, chunks, state=None, groups=(0, 1), last=False):
    first = state is None
    state_shapes = (
        jax.ShapeDtypeStruct((4, HEAD, GROUP * SPAN), jnp.float32),
        jax.ShapeDtypeStruct((4, 8, GROUP * SPAN), jnp.float32),
        jax.ShapeDtypeStruct((4, 8, GROUP * SPAN), jnp.float32),
    )
    vmem, smem = pl.BlockSpec(memory_space=pltpu.VMEM), pl.BlockSpec(memory_space=pltpu.SMEM)
    scratch = [pltpu.VMEM(s.shape, s.dtype) for s in state_shapes] if last else []
    scratch += [
        pltpu.VMEM((4, GROUP * SPAN, HEAD), jnp.bfloat16),
        pltpu.VMEM((1024, HEAD), jnp.bfloat16),
        pltpu.VMEM((HEAD, 1024), jnp.bfloat16),
    ]
    if first:
        scratch += [pltpu.SMEM((SPANS,), jnp.int32), pltpu.SMEM((4, SPANS), jnp.int32)]
    sources = tuple((source, len(pieces)) for source, pieces in chunks)
    if any(pieces > 1 for _, pieces in sources):
        scratch += [pltpu.VMEM((1024, 2 * HEAD), jnp.bfloat16)]
    arrived = [piece for _, pieces in chunks for piece in pieces]
    inputs = [own, other, *arrived, *([] if first else state)]
    if last:
        shapes, specs = jax.ShapeDtypeStruct((4, 32, GROUP * HEAD), jnp.bfloat16), vmem
    else:
        shapes, specs = state_shapes, (vmem,) * 3
        if first:
            shapes, specs = (*shapes, jax.ShapeDtypeStruct((4, 64), jnp.int32)), (*specs, smem)
    pairs = len(sources) * len(groups) * 20 * SPAN * GROUP * SPAN
    return pl.pallas_call(
        functools.partial(kernel, sources, groups, first, last),
        out_shape=shapes,
        in_specs=[smem] + [vmem] * len(inputs),
        out_specs=specs,
        scratch_shapes=scratch,
        compiler_params=pltpu.CompilerParams(vmem_limit_bytes=24 * 1024 * 1024),
        cost_estimate=pl.CostEstimate(
            flops=4 * pairs * HEAD, bytes_accessed=4 * 1024 * 1024, transcendentals=pairs
        ),
    )(plan, *inputs)


def shards(queries, keys, values, span_order):
    core = lax.axis_index("ctx") % 2
    half = GROUP * HEAD
    kv = [
        jnp.concatenate([a[0][:, h * HEAD : (h + 1) * HEAD] for a in (keys, values)], axis=1)
        for h in range(2)
    ]
    q = (queries[0][:, :half], queries[0][:, half:])
    kv_own, kv_other = jnp.where(core == 0, kv[0], kv[1]), jnp.where(core == 0, kv[1], kv[0])
    own, other = jnp.where(core == 0, q[0], q[1]), jnp.where(core == 0, q[1], q[0])
    chip_kv = jnp.concatenate([kv_own, between_cores(kv_other)], axis=0)
    other = between_cores(other)
    planes = [[z * 8 + r for z in range(4)] for r in range(8)]
    column = lax.all_gather(chip_kv, "ctx", axis=0, tiled=True, axis_index_groups=planes)
    column, own, other = lax.optimization_barrier((column, own, other))
    back, ahead = along_x(column, 3), along_x(column, 1)
    straight = along_x(column[:DIRECT], 2)
    *state, plan = attend(span_order, own, other, [(0, [column])])
    back, *state = lax.optimization_barrier((back, *state))
    relayed = along_x(back[DIRECT:], 3)
    state = attend(plan, own, other, [(3, [back]), (1, [ahead])], state)
    last = ([(2, [straight, relayed])], state)
    out_other = between_cores(attend(plan, own, other, *last, groups=(1,), last=True))
    out_own = attend(plan, own, other, *last, groups=(0,), last=True)
    out = jnp.where(
        core == 0,
        jnp.concatenate([out_own, out_other], axis=2),
        jnp.concatenate([out_other, out_own], axis=2),
    )
    pieces = [to_next_section(out[d], d) for d in range(4)]
    vmem = pl.BlockSpec(memory_space=pltpu.VMEM)
    return pl.pallas_call(
        join,
        out_shape=jax.ShapeDtypeStruct((32, 4 * 2 * half), jnp.bfloat16),
        in_specs=[vmem] * 4,
        out_specs=vmem,
        compiler_params=pltpu.CompilerParams(vmem_limit_bytes=4 * 1024 * 1024),
    )(*pieces)[None]


def solution(mesh):
    placed = (P("section", "ctx", "tp"), P("section", "ctx", "tp"), P("section", "ctx", "tp"), P())
    return jax.shard_map(
        shards,
        mesh=mesh,
        in_specs=placed,
        out_specs=P("section", ("ctx", "tp"), None),
        check_vma=False,
    )
```

time: 144 us -> 134 us (0.931)
  starting transfers between devices: 18.7 us -> 54.5 us
  blocking collectives: 72.1 us -> 48.8 us
  waiting for transfers between devices: 29.6 us -> 13 us
  Pallas kernels: 20.2 us -> 16.2 us
  local copies, waits for them, and re-layouts: 2.88 us -> 0.96 us
    ppermute x2 -> x7, starting transfers between devices: 8.76 us -> 41.6 us  [the longest x3 29.6 us: between_cores(): lax.ppermute(array, 'ctx', [(i, i ^ 1) for i in range(lax.axis_size('ctx'...]
    all_to_all x1 -> x0, blocking collectives: 21.2 us -> none  [shards(): lax.all_to_all(out, ('ctx', 'tp'), split_axis=0, concat_axis=0, tiled=Tru...]
    ppermute x2 -> x7, waiting for transfers between devices: 27.3 us -> 12.5 us  [the longest x4 12.4 us: to_next_section(): return lax.ppermute(array, ('section', 'tp'), pairs)]
    pallas_call x4 -> x5, Pallas kernels: 20.2 us -> 16.2 us  [the longest x4 15.4 us: attend(): pl.pallas_call(functools.partial(kernel, sources, groups, first, last), o...]
    ppermute x3 -> x4, starting transfers between devices: 9.92 us -> 12.9 us  [along_x(): return lax.ppermute(array, 'ctx', pairs)]
    all_gather x1, blocking collectives: 50.9 us -> 48.8 us  [shards(): lax.all_gather(chip_kv, 'ctx', axis=0, tiled=True, axis_index_groups=planes)]
    ppermute x3 -> x4, waiting for transfers between devices: 2.33 us -> 0.53 us  [along_x(): return lax.ppermute(array, 'ctx', pairs)]
    reshape x2 -> x0, local copies, waits for them, and re-layouts: 1.73 us -> none  [the longest x1 1.19 us: shards(): return out.reshape(1, 32, 8 * half)]
  transfers between devices with their start and end apart: 5 -> 11, of which waited for: 4 -> 5; matrix products, arithmetic and copies ran while one was open for 0% -> 0% of each run, Pallas kernels for 10% -> 10%
where the time goes in v2:
time: 134 us
  starting transfers between devices  54.5 us (41%)
  blocking collectives  48.8 us (36%)
  Pallas kernels  16.2 us (12%)
  waiting for transfers between devices  13 us (10%)
    all_gather x1, blocking collectives, shards(): lax.all_gather(chip_kv, 'ctx', axis=0, tiled=True, axis_index_groups=planes)  48.8 us
    ppermute x3, starting transfers between devices, between_cores(): lax.ppermute(array, 'ctx', [(i, i ^ 1) for i in range(lax.axis_size('ctx'...  29.6 us
    pallas_call x4, Pallas kernels, attend(): pl.pallas_call(functools.partial(kernel, sources, groups, first, last), o...  15.4 us
    ppermute x4, starting transfers between devices, along_x(): return lax.ppermute(array, 'ctx', pairs)  12.9 us
    ppermute x4, waiting for transfers between devices, to_next_section(): return lax.ppermute(array, ('section', 'tp'), pairs)  12.4 us
    ppermute x4, starting transfers between devices, to_next_section(): return lax.ppermute(array, ('section', 'tp'), pairs)  12 us
  transfers between devices with their start and end apart: 11, of which 5 were waited for; matrix products, arithmetic and copies ran while one was open for 0% of the time, Pallas kernels for 10%

profile of v2, /device:TPU:1, one launch (start us, length us, event | category | flops | bytes accessed | tf_op | source)
XLA Modules:
  0.0 134.0 jit_solution(5463648449774073943)
XLA Ops:
  0.0 0.0 copy-start.1
  0.0 0.9 fusion
  0.9 16.1 %collective-permute-start = (bf16[128,256]{1,0:T(8,128)(2,1)S(1)}, bf16[128,256]{1,0:T(8,128)(2,1)S(1)}, u32[]{:S(2)}, u32[]{:S(2)}) collective-permute-start(bf16[128,256]{1,0:T(8,128)(2,1)S(1)} %get-tuple-element.40), channel_id=1, source_target_pairs={{0,4},{4,0},{8,12},{12,8},{16,20},{20,16},{24,28},{28,24},{32,36},... | collective-permute-start | bytes 196616 | tf_op jit(solution)/shard_map/ppermute | solution.py:23
  17.0 0.0 copy-done.1
  17.0 1.9 %collective-permute-start.1 = (bf16[128,1024]{1,0:T(8,128)(2,1)S(1)}, bf16[128,1024]{1,0:T(8,128)(2,1)S(1)}, u32[]{:S(2)}, u32[]{:S(2)}) collective-permute-start(bf16[128,1024]{1,0:T(8,128)(2,1)S(1)} %get-tuple-element.37), channel_id=1, source_target_pairs={{0,4},{4,0},{8,12},{12,8},{16,20},{20,16},{24,28},{28,24},{32,36},... | collective-permute-start | bytes 786440 | tf_op jit(solution)/shard_map/ppermute | solution.py:23
  19.0 0.0 collective-permute-done
  19.0 48.8 %all_gather.3.refs_3_ = bf16[1024,256]{1,0:T(8,128)(2,1)S(1)} all-gather(bf16[256,256]{1,0:T(8,128)(2,1)S(1)} %pad_maximum_fusion), channel_id=1, replica_groups={{0,32,64,96},{4,36,68,100},{8,40,72,104},{12,44,76,108},{16,48,80,112},..., dimensions={0}, use_global_device_ids=true | all-gather | bytes 655360 | tf_op jit(solution)/shard_map/all_gather | solution.py:262
  67.8 0.0 copy-start
  67.8 0.0 collective-permute-done.1.refs_2_
  67.8 4.5 %collective-permute-start.3 = (bf16[1024,256]{1,0:T(8,128)(2,1)S(1)}, bf16[1024,256]{1,0:T(8,128)(2,1)S(1)}, u32[]{:S(2)}, u32[]{:S(2)}) collective-permute-start(bf16[1024,256]{1,0:T(8,128)(2,1)S(1)} %all_gather.3.refs_3_), channel_id=1, source_target_pairs={{0,24},{4,28},{8,0},{12,4},{16,8},{20,12},{24,16},{28,20},{32,56},... | collective-permute-start | bytes 1572872 | tf_op jit(solution)/shard_map/ppermute | solution.py:38
  72.3 1.9 %collective-permute-start.5 = (bf16[1024,256]{1,0:T(8,128)(2,1)S(1)}, bf16[1024,256]{1,0:T(8,128)(2,1)S(1)}, u32[]{:S(2)}, u32[]{:S(2)}) collective-permute-start(bf16[1024,256]{1,0:T(8,128)(2,1)S(1)} %all_gather.3.refs_3_), channel_id=1, source_target_pairs={{0,8},{4,12},{8,16},{12,20},{16,24},{20,28},{24,0},{28,4},{32,40},... | collective-permute-start | bytes 1572872 | tf_op jit(solution)/shard_map/ppermute | solution.py:38
  74.2 0.0 copy-done
  74.3 5.2 %shard_map.46 = (f32[4,128,512]{2,1,0:T(8,128)S(1)}, f32[4,8,512]{2,1,0:T(8,128)S(1)}, f32[4,8,512]{2,1,0:T(8,128)S(1)}, s32[4,64]{1,0:T(4,128)S(1)}) custom-call(s32[64]{0:T(128)S(1)} %copy-done, bf16[128,1024]{1,0:T(8,128)(2,1)S(1)} %get-tuple-element.19.refs_1_, bf16[128,1024]{1,0:T(8,128)(2,1)S(1)} %collective-permute-done.1.refs_2_, ...), custom_call_target="tpu_custom_call" | custom-call | flops 671088640 | bytes 4194304 | tf_op jit(solution)/shard_map/pallas_call | solution.py:236
  79.4 0.0 collective-permute-done.3.refs_3_
  79.5 4.6 %collective-permute-start.4 = (bf16[640,256]{1,0:T(8,128)(2,1)S(1)}, bf16[640,256]{1,0:T(8,128)(2,1)S(1)}, u32[]{:S(2)}, u32[]{:S(2)}) collective-permute-start(bf16[640,256]{1,0:T(8,128)(2,1)S(1)} %slice.43), channel_id=1, source_target_pairs={{0,24},{4,28},{8,0},{12,4},{16,8},{20,12},{24,16},{28,20},{32,56},... | collective-permute-start | bytes 983048 | tf_op jit(solution)/shard_map/ppermute | solution.py:38
  84.1 1.9 %collective-permute-start.2 = (bf16[384,256]{1,0:T(8,128)(2,1)S(1)}, bf16[384,256]{1,0:T(8,128)(2,1)S(1)}, u32[]{:S(2)}, u32[]{:S(2)}) collective-permute-start(bf16[384,256]{1,0:T(8,128)(2,1)S(1)} %slice.42), channel_id=1, source_target_pairs={{0,16},{4,20},{8,24},{12,28},{16,0},{20,4},{24,8},{28,12},{32,48},... | collective-permute-start | bytes 589832 | tf_op jit(solution)/shard_map/ppermute | solution.py:38
  86.0 0.0 collective-permute-done.5.refs_4_
  86.0 5.8 %shard_map.47 = (f32[4,128,512]{2,1,0:T(8,128)S(1)}, f32[4,8,512]{2,1,0:T(8,128)S(1)}, f32[4,8,512]{2,1,0:T(8,128)S(1)}) custom-call(s32[4,64]{1,0:T(4,128)S(1)} %get-tuple-element.22.refs_0_, bf16[128,1024]{1,0:T(8,128)(2,1)S(1)} %get-tuple-element.19.refs_1_, bf16[128,1024]{1,0:T(8,128)(2,1)S(1)} %collective-permute-done.1.refs_2_, ...), custom_call_target="tpu_custom_call" | custom-call | flops 1342177280 | bytes 4194304 | tf_op jit(solution)/shard_map/pallas_call | solution.py:236
  91.9 0.5 collective-permute-done.2.refs_3_
  92.4 0.0 collective-permute-done.4.refs_4_
  92.4 2.2 %shard_map.49 = bf16[4,32,1024]{2,1,0:T(8,128)(2,1)S(1)} custom-call(s32[4,64]{1,0:T(4,128)S(1)} %get-tuple-element.22.refs_0_, bf16[128,1024]{1,0:T(8,128)(2,1)S(1)} %get-tuple-element.19.refs_1_, bf16[128,1024]{1,0:T(8,128)(2,1)S(1)} %collective-permute-done.1.refs_2_, bf16[384,256]{1,0:T(8,128)(2,1)S(1)} %collective-permute-done.2.refs_3_, ...), custom_call_target="tpu_custom_call" | custom-call | flops 335544320 | bytes 4194304 | tf_op jit(solution)/shard_map/pallas_call | solution.py:236
  94.6 11.6 %collective-permute-start.6 = (bf16[4,32,1024]{2,1,0:T(8,128)(2,1)S(1)}, bf16[4,32,1024]{2,1,0:T(8,128)(2,1)S(1)}, u32[]{:S(2)}, u32[]{:S(2)}) collective-permute-start(bf16[4,32,1024]{2,1,0:T(8,128)(2,1)S(1)} %shard_map.49), channel_id=1, source_target_pairs={{0,4},{4,0},{8,12},{12,8},{16,20},{20,16},{24,28},{28,24},{32,36},... | collective-permute-start | bytes 786440 | tf_op jit(solution)/shard_map/ppermute | solution.py:23
  106.2 2.2 %shard_map.48 = bf16[4,32,1024]{2,1,0:T(8,128)(2,1)S(1)} custom-call(s32[4,64]{1,0:T(4,128)S(1)} %get-tuple-element.22.refs_0_, bf16[128,1024]{1,0:T(8,128)(2,1)S(1)} %get-tuple-element.19.refs_1_, bf16[128,1024]{1,0:T(8,128)(2,1)S(1)} %collective-permute-done.1.refs_2_, bf16[384,256]{1,0:T(8,128)(2,1)S(1)} %collective-permute-done.2.refs_3_, ...), custom_call_target="tpu_custom_call" | custom-call | flops 335544320 | bytes 4194304 | tf_op jit(solution)/shard_map/pallas_call | solution.py:236
  108.4 0.0 collective-permute-done.6
  108.4 0.1 maximum_select_fusion
  108.6 1.9 %collective-permute-start.10 = (bf16[32,2048]{1,0:T(8,128)(2,1)S(1)}, bf16[32,2048]{1,0:T(8,128)(2,1)S(1)}, u32[]{:S(2)}, u32[]{:S(2)}) collective-permute-start(bf16[32,2048]{1,0:T(8,128)(2,1)S(1)} %get-tuple-element.33), channel_id=1, source_target_pairs={{0,131},{1,128},{2,129},{3,130},{128,259},{129,256},{130,257},{131... | collective-permute-start | bytes 393224 | tf_op jit(solution)/shard_map/ppermute | solution.py:33
  110.6 1.9 %collective-permute-start.9 = (bf16[32,2048]{1,0:T(8,128)(2,1)S(1)}, bf16[32,2048]{1,0:T(8,128)(2,1)S(1)}, u32[]{:S(2)}, u32[]{:S(2)}) collective-permute-start(bf16[32,2048]{1,0:T(8,128)(2,1)S(1)} %get-tuple-element.34), channel_id=1, source_target_pairs={{0,130},{1,131},{2,128},{3,129},{128,258},{129,259},{130,256},{131... | collective-permute-start | bytes 393224 | tf_op jit(solution)/shard_map/ppermute | solution.py:33
  112.5 1.9 %collective-permute-start.8 = (bf16[32,2048]{1,0:T(8,128)(2,1)S(1)}, bf16[32,2048]{1,0:T(8,128)(2,1)S(1)}, u32[]{:S(2)}, u32[]{:S(2)}) collective-permute-start(bf16[32,2048]{1,0:T(8,128)(2,1)S(1)} %get-tuple-element.35), channel_id=1, source_target_pairs={{0,129},{1,130},{2,131},{3,128},{128,257},{129,258},{130,259},{131... | collective-permute-start | bytes 393224 | tf_op jit(solution)/shard_map/ppermute | solution.py:33
  114.4 6.2 %collective-permute-start.7 = (bf16[32,2048]{1,0:T(8,128)(2,1)S(1)}, bf16[32,2048]{1,0:T(8,128)(2,1)S(1)}, u32[]{:S(2)}, u32[]{:S(2)}) collective-permute-start(bf16[32,2048]{1,0:T(8,128)(2,1)S(1)} %get-tuple-element.36), channel_id=1, source_target_pairs={{0,128},{1,129},{2,130},{3,131},{128,256},{129,257},{130,258},{131... | collective-permute-start | bytes 393224 | tf_op jit(solution)/shard_map/ppermute | solution.py:33
  120.7 2.5 %collective-permute-done.10.refs_3_ = bf16[32,2048]{1,0:T(8,128)(2,1)S(1)} collective-permute-done((bf16[32,2048]{1,0:T(8,128)(2,1)S(1)}, bf16[32,2048]{1,0:T(8,128)(2,1)S(1)}, u32[]{:S(2)}, u32[]{:S(2)}) %collective-permute-start.10) | collective-permute-done | bytes 131104 | tf_op jit(solution)/shard_map/ppermute | solution.py:33
  123.1 4.4 %collective-permute-done.9.refs_2_ = bf16[32,2048]{1,0:T(8,128)(2,1)S(1)} collective-permute-done((bf16[32,2048]{1,0:T(8,128)(2,1)S(1)}, bf16[32,2048]{1,0:T(8,128)(2,1)S(1)}, u32[]{:S(2)}, u32[]{:S(2)}) %collective-permute-start.9) | collective-permute-done | bytes 131104 | tf_op jit(solution)/shard_map/ppermute | solution.py:33
  127.6 3.0 %collective-permute-done.8.refs_1_ = bf16[32,2048]{1,0:T(8,128)(2,1)S(1)} collective-permute-done((bf16[32,2048]{1,0:T(8,128)(2,1)S(1)}, bf16[32,2048]{1,0:T(8,128)(2,1)S(1)}, u32[]{:S(2)}, u32[]{:S(2)}) %collective-permute-start.8) | collective-permute-done | bytes 131104 | tf_op jit(solution)/shard_map/ppermute | solution.py:33
  130.6 2.5 %collective-permute-done.7.refs_0_ = bf16[32,2048]{1,0:T(8,128)(2,1)S(1)} collective-permute-done((bf16[32,2048]{1,0:T(8,128)(2,1)S(1)}, bf16[32,2048]{1,0:T(8,128)(2,1)S(1)}, u32[]{:S(2)}, u32[]{:S(2)}) %collective-permute-start.7) | collective-permute-done | bytes 131104 | tf_op jit(solution)/shard_map/ppermute | solution.py:33
  133.1 0.8 shard_map.50
  (6 shorter events, 0.2 us)
Async XLA Ops:
  0.0 17.0 %copy-start.1 = (bf16[1,128,2048]{2,1,0:T(8,128)(2,1)S(1)}, bf16[1,128,2048]{2,1,0:T(8,128)(2,1)}, u32[]{:S(2)}) copy-start(bf16[1,128,2048]{2,1,0:T(8,128)(2,1)} %param.4) | copy-start | bytes 1572868
  0.9 18.1 %collective-permute-start = (bf16[128,256]{1,0:T(8,128)(2,1)S(1)}, bf16[128,256]{1,0:T(8,128)(2,1)S(1)}, u32[]{:S(2)}, u32[]{:S(2)}) collective-permute-start(bf16[128,256]{1,0:T(8,128)(2,1)S(1)} %get-tuple-element.40), channel_id=1, source_target_pairs={{0,4},{4,0},{8,12},{12,8},{16,20},{20,16},{24,28},{28,24},{32,36},... | collective-permute-start | bytes 196616 | tf_op jit(solution)/shard_map/ppermute | solution.py:23
  17.0 50.7 %collective-permute-start.1 = (bf16[128,1024]{1,0:T(8,128)(2,1)S(1)}, bf16[128,1024]{1,0:T(8,128)(2,1)S(1)}, u32[]{:S(2)}, u32[]{:S(2)}) collective-permute-start(bf16[128,1024]{1,0:T(8,128)(2,1)S(1)} %get-tuple-element.37), channel_id=1, source_target_pairs={{0,4},{4,0},{8,12},{12,8},{16,20},{20,16},{24,28},{28,24},{32,36},... | collective-permute-start | bytes 786440 | tf_op jit(solution)/shard_map/ppermute | solution.py:23
  67.8 6.5 %copy-start = (s32[64]{0:T(128)S(1)}, s32[64]{0:T(128)}, u32[]{:S(2)}) copy-start(s32[64]{0:T(128)} %refs_0_.1) | copy-start | bytes 772
  67.8 11.6 %collective-permute-start.3 = (bf16[1024,256]{1,0:T(8,128)(2,1)S(1)}, bf16[1024,256]{1,0:T(8,128)(2,1)S(1)}, u32[]{:S(2)}, u32[]{:S(2)}) collective-permute-start(bf16[1024,256]{1,0:T(8,128)(2,1)S(1)} %all_gather.3.refs_3_), channel_id=1, source_target_pairs={{0,24},{4,28},{8,0},{12,4},{16,8},{20,12},{24,16},{28,20},{32,56},... | collective-permute-start | bytes 1572872 | tf_op jit(solution)/shard_map/ppermute | solution.py:38
  72.3 13.7 %collective-permute-start.5 = (bf16[1024,256]{1,0:T(8,128)(2,1)S(1)}, bf16[1024,256]{1,0:T(8,128)(2,1)S(1)}, u32[]{:S(2)}, u32[]{:S(2)}) collective-permute-start(bf16[1024,256]{1,0:T(8,128)(2,1)S(1)} %all_gather.3.refs_3_), channel_id=1, source_target_pairs={{0,8},{4,12},{8,16},{12,20},{16,24},{20,28},{24,0},{28,4},{32,40},... | collective-permute-start | bytes 1572872 | tf_op jit(solution)/shard_map/ppermute | solution.py:38
  79.5 12.9 %collective-permute-start.4 = (bf16[640,256]{1,0:T(8,128)(2,1)S(1)}, bf16[640,256]{1,0:T(8,128)(2,1)S(1)}, u32[]{:S(2)}, u32[]{:S(2)}) collective-permute-start(bf16[640,256]{1,0:T(8,128)(2,1)S(1)} %slice.43), channel_id=1, source_target_pairs={{0,24},{4,28},{8,0},{12,4},{16,8},{20,12},{24,16},{28,20},{32,56},... | collective-permute-start | bytes 983048 | tf_op jit(solution)/shard_map/ppermute | solution.py:38
  84.1 8.3 %collective-permute-start.2 = (bf16[384,256]{1,0:T(8,128)(2,1)S(1)}, bf16[384,256]{1,0:T(8,128)(2,1)S(1)}, u32[]{:S(2)}, u32[]{:S(2)}) collective-permute-start(bf16[384,256]{1,0:T(8,128)(2,1)S(1)} %slice.42), channel_id=1, source_target_pairs={{0,16},{4,20},{8,24},{12,28},{16,0},{20,4},{24,8},{28,12},{32,48},... | collective-permute-start | bytes 589832 | tf_op jit(solution)/shard_map/ppermute | solution.py:38
  94.6 13.8 %collective-permute-start.6 = (bf16[4,32,1024]{2,1,0:T(8,128)(2,1)S(1)}, bf16[4,32,1024]{2,1,0:T(8,128)(2,1)S(1)}, u32[]{:S(2)}, u32[]{:S(2)}) collective-permute-start(bf16[4,32,1024]{2,1,0:T(8,128)(2,1)S(1)} %shard_map.49), channel_id=1, source_target_pairs={{0,4},{4,0},{8,12},{12,8},{16,20},{20,16},{24,28},{28,24},{32,36},... | collective-permute-start | bytes 786440 | tf_op jit(solution)/shard_map/ppermute | solution.py:23
  108.6 14.5 %collective-permute-start.10 = (bf16[32,2048]{1,0:T(8,128)(2,1)S(1)}, bf16[32,2048]{1,0:T(8,128)(2,1)S(1)}, u32[]{:S(2)}, u32[]{:S(2)}) collective-permute-start(bf16[32,2048]{1,0:T(8,128)(2,1)S(1)} %get-tuple-element.33), channel_id=1, source_target_pairs={{0,131},{1,128},{2,129},{3,130},{128,259},{129,256},{130,257},{131... | collective-permute-start | bytes 393224 | tf_op jit(solution)/shard_map/ppermute | solution.py:33
  110.6 17.0 %collective-permute-start.9 = (bf16[32,2048]{1,0:T(8,128)(2,1)S(1)}, bf16[32,2048]{1,0:T(8,128)(2,1)S(1)}, u32[]{:S(2)}, u32[]{:S(2)}) collective-permute-start(bf16[32,2048]{1,0:T(8,128)(2,1)S(1)} %get-tuple-element.34), channel_id=1, source_target_pairs={{0,130},{1,131},{2,128},{3,129},{128,258},{129,259},{130,256},{131... | collective-permute-start | bytes 393224 | tf_op jit(solution)/shard_map/ppermute | solution.py:33
  112.5 18.1 %collective-permute-start.8 = (bf16[32,2048]{1,0:T(8,128)(2,1)S(1)}, bf16[32,2048]{1,0:T(8,128)(2,1)S(1)}, u32[]{:S(2)}, u32[]{:S(2)}) collective-permute-start(bf16[32,2048]{1,0:T(8,128)(2,1)S(1)} %get-tuple-element.35), channel_id=1, source_target_pairs={{0,129},{1,130},{2,131},{3,128},{128,257},{129,258},{130,259},{131... | collective-permute-start | bytes 393224 | tf_op jit(solution)/shard_map/ppermute | solution.py:33
  114.4 18.7 %collective-permute-start.7 = (bf16[32,2048]{1,0:T(8,128)(2,1)S(1)}, bf16[32,2048]{1,0:T(8,128)(2,1)S(1)}, u32[]{:S(2)}, u32[]{:S(2)}) collective-permute-start(bf16[32,2048]{1,0:T(8,128)(2,1)S(1)} %get-tuple-element.36), channel_id=1, source_target_pairs={{0,128},{1,129},{2,130},{3,131},{128,256},{129,257},{130,258},{131... | collective-permute-start | bytes 393224 | tf_op jit(solution)/shard_map/ppermute | solution.py:33

commit v3 on v2

--- a/solution.py
+++ b/solution.py
@@ -46,7 +46,7 @@
         held_by[order[i]] = i
         return carry
 
-    lax.fori_loop(0, SPANS, place, 0, unroll=8)
+    lax.fori_loop(0, SPANS, place, 0, unroll=32)
 
     def sort(p, filled):
         i = held_by[p]
@@ -60,7 +60,7 @@
             counts[d, p] = updated[d]
         return tuple(updated)
 
-    lax.fori_loop(0, SPANS, sort, (jnp.int32(0),) * 4, unroll=4)
+    lax.fori_loop(0, SPANS, sort, (jnp.int32(0),) * 4, unroll=16)
     for j in range(2):
         owner = ctx if j == 0 else ctx + 1 - 2 * my_core
         for e in range(2):
@@ -98,7 +98,7 @@
         total[...] = jnp.zeros_like(total)
     else:
         for j in groups:
-            for ref, given in ((acc, acc_in), (top, top_in), (total, total_in)):
+            for ref, given in ((top, top_in), (total, total_in)):
                 ref[2 * j : 2 * j + 2] = given[2 * j : 2 * j + 2]
 
     width = GROUP * SPAN
@@ -107,7 +107,8 @@
         query_row = lax.broadcasted_iota(jnp.int32, (SPAN, width), 1) % SPAN
         later_by = key_row - query_row
 
-    for (source, pieces), chunk in zip(sources, chunks):
+    for n, ((source, pieces), chunk) in enumerate(zip(sources, chunks)):
+        held = acc if first or n > 0 else acc_in
         if pieces == 1:
             chunk = chunk[0]
         else:
@@ -169,7 +170,8 @@
                 fade.append(jnp.exp2((before - new) * SCALE))
             for e in range(2):
                 s = 2 * j + e
-                acc[s] = (acc[s].reshape(HEAD // 8, 8, width) * fade[e][None]).reshape(HEAD, width)
+                faded = held[s].reshape(HEAD // 8, 8, width) * fade[e][None]
+                acc[s] = faded.reshape(HEAD, width)
                 total[s] = total[s] * fade[e]
             for t in range(5):
                 weights, added = [], jnp.zeros((8, width), jnp.float32)

time: 134 us -> 134 us (level)
  no operation moved by 1% of the time
where the time goes in v3:
time: 134 us
  starting transfers between devices  54.5 us (41%)
  blocking collectives  48.8 us (36%)
  Pallas kernels  16.1 us (12%)
  waiting for transfers between devices  13.2 us (10%)
    all_gather x1, blocking collectives, shards(): lax.all_gather(chip_kv, 'ctx', axis=0, tiled=True, axis_index_groups=planes)  48.8 us
    ppermute x3, starting transfers between devices, between_cores(): lax.ppermute(array, 'ctx', [(i, i ^ 1) for i in range(lax.axis_size('ctx'...  29.7 us
    pallas_call x4, Pallas kernels, attend(): pl.pallas_call(functools.partial(kernel, sources, groups, first, last), o...  15.3 us
    ppermute x4, starting transfers between devices, along_x(): return lax.ppermute(array, 'ctx', pairs)  12.9 us
    ppermute x4, waiting for transfers between devices, to_next_section(): return lax.ppermute(array, ('section', 'tp'), pairs)  12.5 us
    ppermute x4, starting transfers between devices, to_next_section(): return lax.ppermute(array, ('section', 'tp'), pairs)  11.9 us
  transfers between devices with their start and end apart: 11, of which 5 were waited for; matrix products, arithmetic and copies ran while one was open for 0% of the time, Pallas kernels for 10%

profile of v3, /device:TPU:1, one launch (start us, length us, event | category | flops | bytes accessed | tf_op | source)
XLA Modules:
  0.0 134.1 jit_solution(10173457539595661429)
XLA Ops:
  0.0 0.0 copy-start.1
  0.0 0.9 fusion
  0.9 16.1 %collective-permute-start = (bf16[128,256]{1,0:T(8,128)(2,1)S(1)}, bf16[128,256]{1,0:T(8,128)(2,1)S(1)}, u32[]{:S(2)}, u32[]{:S(2)}) collective-permute-start(bf16[128,256]{1,0:T(8,128)(2,1)S(1)} %get-tuple-element.40), channel_id=1, source_target_pairs={{0,4},{4,0},{8,12},{12,8},{16,20},{20,16},{24,28},{28,24},{32,36},... | collective-permute-start | bytes 196616 | tf_op jit(solution)/shard_map/ppermute | solution.py:23
  17.0 0.0 copy-done.1
  17.0 1.9 %collective-permute-start.1 = (bf16[128,1024]{1,0:T(8,128)(2,1)S(1)}, bf16[128,1024]{1,0:T(8,128)(2,1)S(1)}, u32[]{:S(2)}, u32[]{:S(2)}) collective-permute-start(bf16[128,1024]{1,0:T(8,128)(2,1)S(1)} %get-tuple-element.37), channel_id=1, source_target_pairs={{0,4},{4,0},{8,12},{12,8},{16,20},{20,16},{24,28},{28,24},{32,36},... | collective-permute-start | bytes 786440 | tf_op jit(solution)/shard_map/ppermute | solution.py:23
  19.0 0.0 collective-permute-done
  19.0 48.8 %all_gather.3.refs_3_ = bf16[1024,256]{1,0:T(8,128)(2,1)S(1)} all-gather(bf16[256,256]{1,0:T(8,128)(2,1)S(1)} %pad_maximum_fusion), channel_id=1, replica_groups={{0,32,64,96},{4,36,68,100},{8,40,72,104},{12,44,76,108},{16,48,80,112},..., dimensions={0}, use_global_device_ids=true | all-gather | bytes 655360 | tf_op jit(solution)/shard_map/all_gather | solution.py:264
  67.8 0.0 copy-start
  67.8 0.0 collective-permute-done.1.refs_2_
  67.8 4.5 %collective-permute-start.3 = (bf16[1024,256]{1,0:T(8,128)(2,1)S(1)}, bf16[1024,256]{1,0:T(8,128)(2,1)S(1)}, u32[]{:S(2)}, u32[]{:S(2)}) collective-permute-start(bf16[1024,256]{1,0:T(8,128)(2,1)S(1)} %all_gather.3.refs_3_), channel_id=1, source_target_pairs={{0,24},{4,28},{8,0},{12,4},{16,8},{20,12},{24,16},{28,20},{32,56},... | collective-permute-start | bytes 1572872 | tf_op jit(solution)/shard_map/ppermute | solution.py:38
  72.3 1.9 %collective-permute-start.5 = (bf16[1024,256]{1,0:T(8,128)(2,1)S(1)}, bf16[1024,256]{1,0:T(8,128)(2,1)S(1)}, u32[]{:S(2)}, u32[]{:S(2)}) collective-permute-start(bf16[1024,256]{1,0:T(8,128)(2,1)S(1)} %all_gather.3.refs_3_), channel_id=1, source_target_pairs={{0,8},{4,12},{8,16},{12,20},{16,24},{20,28},{24,0},{28,4},{32,40},... | collective-permute-start | bytes 1572872 | tf_op jit(solution)/shard_map/ppermute | solution.py:38
  74.2 0.0 copy-done
  74.3 5.1 %shard_map.46 = (f32[4,128,512]{2,1,0:T(8,128)S(1)}, f32[4,8,512]{2,1,0:T(8,128)S(1)}, f32[4,8,512]{2,1,0:T(8,128)S(1)}, s32[4,64]{1,0:T(4,128)S(1)}) custom-call(s32[64]{0:T(128)S(1)} %copy-done, bf16[128,1024]{1,0:T(8,128)(2,1)S(1)} %get-tuple-element.19.refs_1_, bf16[128,1024]{1,0:T(8,128)(2,1)S(1)} %collective-permute-done.1.refs_2_, ...), custom_call_target="tpu_custom_call" | custom-call | flops 671088640 | bytes 4194304 | tf_op jit(solution)/shard_map/pallas_call | solution.py:238
  79.4 0.0 collective-permute-done.3.refs_3_
  79.4 4.6 %collective-permute-start.4 = (bf16[640,256]{1,0:T(8,128)(2,1)S(1)}, bf16[640,256]{1,0:T(8,128)(2,1)S(1)}, u32[]{:S(2)}, u32[]{:S(2)}) collective-permute-start(bf16[640,256]{1,0:T(8,128)(2,1)S(1)} %slice.43), channel_id=1, source_target_pairs={{0,24},{4,28},{8,0},{12,4},{16,8},{20,12},{24,16},{28,20},{32,56},... | collective-permute-start | bytes 983048 | tf_op jit(solution)/shard_map/ppermute | solution.py:38
  84.0 1.9 %collective-permute-start.2 = (bf16[384,256]{1,0:T(8,128)(2,1)S(1)}, bf16[384,256]{1,0:T(8,128)(2,1)S(1)}, u32[]{:S(2)}, u32[]{:S(2)}) collective-permute-start(bf16[384,256]{1,0:T(8,128)(2,1)S(1)} %slice.42), channel_id=1, source_target_pairs={{0,16},{4,20},{8,24},{12,28},{16,0},{20,4},{24,8},{28,12},{32,48},... | collective-permute-start | bytes 589832 | tf_op jit(solution)/shard_map/ppermute | solution.py:38
  85.9 0.0 collective-permute-done.5.refs_4_
  85.9 5.8 %shard_map.47 = (f32[4,128,512]{2,1,0:T(8,128)S(1)}, f32[4,8,512]{2,1,0:T(8,128)S(1)}, f32[4,8,512]{2,1,0:T(8,128)S(1)}) custom-call(s32[4,64]{1,0:T(4,128)S(1)} %get-tuple-element.22.refs_0_, bf16[128,1024]{1,0:T(8,128)(2,1)S(1)} %get-tuple-element.19.refs_1_, bf16[128,1024]{1,0:T(8,128)(2,1)S(1)} %collective-permute-done.1.refs_2_, ...), custom_call_target="tpu_custom_call" | custom-call | flops 1342177280 | bytes 4194304 | tf_op jit(solution)/shard_map/pallas_call | solution.py:238
  91.7 0.6 collective-permute-done.2.refs_3_
  92.4 0.0 collective-permute-done.4.refs_4_
  92.4 2.2 %shard_map.49 = bf16[4,32,1024]{2,1,0:T(8,128)(2,1)S(1)} custom-call(s32[4,64]{1,0:T(4,128)S(1)} %get-tuple-element.22.refs_0_, bf16[128,1024]{1,0:T(8,128)(2,1)S(1)} %get-tuple-element.19.refs_1_, bf16[128,1024]{1,0:T(8,128)(2,1)S(1)} %collective-permute-done.1.refs_2_, bf16[384,256]{1,0:T(8,128)(2,1)S(1)} %collective-permute-done.2.refs_3_, ...), custom_call_target="tpu_custom_call" | custom-call | flops 335544320 | bytes 4194304 | tf_op jit(solution)/shard_map/pallas_call | solution.py:238
  94.6 11.7 %collective-permute-start.6 = (bf16[4,32,1024]{2,1,0:T(8,128)(2,1)S(1)}, bf16[4,32,1024]{2,1,0:T(8,128)(2,1)S(1)}, u32[]{:S(2)}, u32[]{:S(2)}) collective-permute-start(bf16[4,32,1024]{2,1,0:T(8,128)(2,1)S(1)} %shard_map.49), channel_id=1, source_target_pairs={{0,4},{4,0},{8,12},{12,8},{16,20},{20,16},{24,28},{28,24},{32,36},... | collective-permute-start | bytes 786440 | tf_op jit(solution)/shard_map/ppermute | solution.py:23
  106.3 2.2 %shard_map.48 = bf16[4,32,1024]{2,1,0:T(8,128)(2,1)S(1)} custom-call(s32[4,64]{1,0:T(4,128)S(1)} %get-tuple-element.22.refs_0_, bf16[128,1024]{1,0:T(8,128)(2,1)S(1)} %get-tuple-element.19.refs_1_, bf16[128,1024]{1,0:T(8,128)(2,1)S(1)} %collective-permute-done.1.refs_2_, bf16[384,256]{1,0:T(8,128)(2,1)S(1)} %collective-permute-done.2.refs_3_, ...), custom_call_target="tpu_custom_call" | custom-call | flops 335544320 | bytes 4194304 | tf_op jit(solution)/shard_map/pallas_call | solution.py:238
  108.5 0.0 collective-permute-done.6
  108.5 0.1 maximum_select_fusion
  108.7 1.9 %collective-permute-start.10 = (bf16[32,2048]{1,0:T(8,128)(2,1)S(1)}, bf16[32,2048]{1,0:T(8,128)(2,1)S(1)}, u32[]{:S(2)}, u32[]{:S(2)}) collective-permute-start(bf16[32,2048]{1,0:T(8,128)(2,1)S(1)} %get-tuple-element.33), channel_id=1, source_target_pairs={{0,131},{1,128},{2,129},{3,130},{128,259},{129,256},{130,257},{131... | collective-permute-start | bytes 393224 | tf_op jit(solution)/shard_map/ppermute | solution.py:33
  110.7 1.9 %collective-permute-start.9 = (bf16[32,2048]{1,0:T(8,128)(2,1)S(1)}, bf16[32,2048]{1,0:T(8,128)(2,1)S(1)}, u32[]{:S(2)}, u32[]{:S(2)}) collective-permute-start(bf16[32,2048]{1,0:T(8,128)(2,1)S(1)} %get-tuple-element.34), channel_id=1, source_target_pairs={{0,130},{1,131},{2,128},{3,129},{128,258},{129,259},{130,256},{131... | collective-permute-start | bytes 393224 | tf_op jit(solution)/shard_map/ppermute | solution.py:33
  112.6 1.9 %collective-permute-start.8 = (bf16[32,2048]{1,0:T(8,128)(2,1)S(1)}, bf16[32,2048]{1,0:T(8,128)(2,1)S(1)}, u32[]{:S(2)}, u32[]{:S(2)}) collective-permute-start(bf16[32,2048]{1,0:T(8,128)(2,1)S(1)} %get-tuple-element.35), channel_id=1, source_target_pairs={{0,129},{1,130},{2,131},{3,128},{128,257},{129,258},{130,259},{131... | collective-permute-start | bytes 393224 | tf_op jit(solution)/shard_map/ppermute | solution.py:33
  114.5 6.1 %collective-permute-start.7 = (bf16[32,2048]{1,0:T(8,128)(2,1)S(1)}, bf16[32,2048]{1,0:T(8,128)(2,1)S(1)}, u32[]{:S(2)}, u32[]{:S(2)}) collective-permute-start(bf16[32,2048]{1,0:T(8,128)(2,1)S(1)} %get-tuple-element.36), channel_id=1, source_target_pairs={{0,128},{1,129},{2,130},{3,131},{128,256},{129,257},{130,258},{131... | collective-permute-start | bytes 393224 | tf_op jit(solution)/shard_map/ppermute | solution.py:33
  120.7 2.6 %collective-permute-done.10.refs_3_ = bf16[32,2048]{1,0:T(8,128)(2,1)S(1)} collective-permute-done((bf16[32,2048]{1,0:T(8,128)(2,1)S(1)}, bf16[32,2048]{1,0:T(8,128)(2,1)S(1)}, u32[]{:S(2)}, u32[]{:S(2)}) %collective-permute-start.10) | collective-permute-done | bytes 131104 | tf_op jit(solution)/shard_map/ppermute | solution.py:33
  123.2 4.4 %collective-permute-done.9.refs_2_ = bf16[32,2048]{1,0:T(8,128)(2,1)S(1)} collective-permute-done((bf16[32,2048]{1,0:T(8,128)(2,1)S(1)}, bf16[32,2048]{1,0:T(8,128)(2,1)S(1)}, u32[]{:S(2)}, u32[]{:S(2)}) %collective-permute-start.9) | collective-permute-done | bytes 131104 | tf_op jit(solution)/shard_map/ppermute | solution.py:33
  127.7 3.0 %collective-permute-done.8.refs_1_ = bf16[32,2048]{1,0:T(8,128)(2,1)S(1)} collective-permute-done((bf16[32,2048]{1,0:T(8,128)(2,1)S(1)}, bf16[32,2048]{1,0:T(8,128)(2,1)S(1)}, u32[]{:S(2)}, u32[]{:S(2)}) %collective-permute-start.8) | collective-permute-done | bytes 131104 | tf_op jit(solution)/shard_map/ppermute | solution.py:33
  130.7 2.6 %collective-permute-done.7.refs_0_ = bf16[32,2048]{1,0:T(8,128)(2,1)S(1)} collective-permute-done((bf16[32,2048]{1,0:T(8,128)(2,1)S(1)}, bf16[32,2048]{1,0:T(8,128)(2,1)S(1)}, u32[]{:S(2)}, u32[]{:S(2)}) %collective-permute-start.7) | collective-permute-done | bytes 131104 | tf_op jit(solution)/shard_map/ppermute | solution.py:33
  133.2 0.8 shard_map.50
  (6 shorter events, 0.2 us)
Async XLA Ops:
  0.0 17.0 %copy-start.1 = (bf16[1,128,2048]{2,1,0:T(8,128)(2,1)S(1)}, bf16[1,128,2048]{2,1,0:T(8,128)(2,1)}, u32[]{:S(2)}) copy-start(bf16[1,128,2048]{2,1,0:T(8,128)(2,1)} %param.4) | copy-start | bytes 1572868
  0.9 18.1 %collective-permute-start = (bf16[128,256]{1,0:T(8,128)(2,1)S(1)}, bf16[128,256]{1,0:T(8,128)(2,1)S(1)}, u32[]{:S(2)}, u32[]{:S(2)}) collective-permute-start(bf16[128,256]{1,0:T(8,128)(2,1)S(1)} %get-tuple-element.40), channel_id=1, source_target_pairs={{0,4},{4,0},{8,12},{12,8},{16,20},{20,16},{24,28},{28,24},{32,36},... | collective-permute-start | bytes 196616 | tf_op jit(solution)/shard_map/ppermute | solution.py:23
  17.0 50.7 %collective-permute-start.1 = (bf16[128,1024]{1,0:T(8,128)(2,1)S(1)}, bf16[128,1024]{1,0:T(8,128)(2,1)S(1)}, u32[]{:S(2)}, u32[]{:S(2)}) collective-permute-start(bf16[128,1024]{1,0:T(8,128)(2,1)S(1)} %get-tuple-element.37), channel_id=1, source_target_pairs={{0,4},{4,0},{8,12},{12,8},{16,20},{20,16},{24,28},{28,24},{32,36},... | collective-permute-start | bytes 786440 | tf_op jit(solution)/shard_map/ppermute | solution.py:23
  67.8 6.5 %copy-start = (s32[64]{0:T(128)S(1)}, s32[64]{0:T(128)}, u32[]{:S(2)}) copy-start(s32[64]{0:T(128)} %refs_0_.1) | copy-start | bytes 772
  67.8 11.6 %collective-permute-start.3 = (bf16[1024,256]{1,0:T(8,128)(2,1)S(1)}, bf16[1024,256]{1,0:T(8,128)(2,1)S(1)}, u32[]{:S(2)}, u32[]{:S(2)}) collective-permute-start(bf16[1024,256]{1,0:T(8,128)(2,1)S(1)} %all_gather.3.refs_3_), channel_id=1, source_target_pairs={{0,24},{4,28},{8,0},{12,4},{16,8},{20,12},{24,16},{28,20},{32,56},... | collective-permute-start | bytes 1572872 | tf_op jit(solution)/shard_map/ppermute | solution.py:38
  72.3 13.6 %collective-permute-start.5 = (bf16[1024,256]{1,0:T(8,128)(2,1)S(1)}, bf16[1024,256]{1,0:T(8,128)(2,1)S(1)}, u32[]{:S(2)}, u32[]{:S(2)}) collective-permute-start(bf16[1024,256]{1,0:T(8,128)(2,1)S(1)} %all_gather.3.refs_3_), channel_id=1, source_target_pairs={{0,8},{4,12},{8,16},{12,20},{16,24},{20,28},{24,0},{28,4},{32,40},... | collective-permute-start | bytes 1572872 | tf_op jit(solution)/shard_map/ppermute | solution.py:38
  79.4 13.0 %collective-permute-start.4 = (bf16[640,256]{1,0:T(8,128)(2,1)S(1)}, bf16[640,256]{1,0:T(8,128)(2,1)S(1)}, u32[]{:S(2)}, u32[]{:S(2)}) collective-permute-start(bf16[640,256]{1,0:T(8,128)(2,1)S(1)} %slice.43), channel_id=1, source_target_pairs={{0,24},{4,28},{8,0},{12,4},{16,8},{20,12},{24,16},{28,20},{32,56},... | collective-permute-start | bytes 983048 | tf_op jit(solution)/shard_map/ppermute | solution.py:38
  84.0 8.4 %collective-permute-start.2 = (bf16[384,256]{1,0:T(8,128)(2,1)S(1)}, bf16[384,256]{1,0:T(8,128)(2,1)S(1)}, u32[]{:S(2)}, u32[]{:S(2)}) collective-permute-start(bf16[384,256]{1,0:T(8,128)(2,1)S(1)} %slice.42), channel_id=1, source_target_pairs={{0,16},{4,20},{8,24},{12,28},{16,0},{20,4},{24,8},{28,12},{32,48},... | collective-permute-start | bytes 589832 | tf_op jit(solution)/shard_map/ppermute | solution.py:38
  94.6 13.9 %collective-permute-start.6 = (bf16[4,32,1024]{2,1,0:T(8,128)(2,1)S(1)}, bf16[4,32,1024]{2,1,0:T(8,128)(2,1)S(1)}, u32[]{:S(2)}, u32[]{:S(2)}) collective-permute-start(bf16[4,32,1024]{2,1,0:T(8,128)(2,1)S(1)} %shard_map.49), channel_id=1, source_target_pairs={{0,4},{4,0},{8,12},{12,8},{16,20},{20,16},{24,28},{28,24},{32,36},... | collective-permute-start | bytes 786440 | tf_op jit(solution)/shard_map/ppermute | solution.py:23
  108.7 14.5 %collective-permute-start.10 = (bf16[32,2048]{1,0:T(8,128)(2,1)S(1)}, bf16[32,2048]{1,0:T(8,128)(2,1)S(1)}, u32[]{:S(2)}, u32[]{:S(2)}) collective-permute-start(bf16[32,2048]{1,0:T(8,128)(2,1)S(1)} %get-tuple-element.33), channel_id=1, source_target_pairs={{0,131},{1,128},{2,129},{3,130},{128,259},{129,256},{130,257},{131... | collective-permute-start | bytes 393224 | tf_op jit(solution)/shard_map/ppermute | solution.py:33
  110.7 17.0 %collective-permute-start.9 = (bf16[32,2048]{1,0:T(8,128)(2,1)S(1)}, bf16[32,2048]{1,0:T(8,128)(2,1)S(1)}, u32[]{:S(2)}, u32[]{:S(2)}) collective-permute-start(bf16[32,2048]{1,0:T(8,128)(2,1)S(1)} %get-tuple-element.34), channel_id=1, source_target_pairs={{0,130},{1,131},{2,128},{3,129},{128,258},{129,259},{130,256},{131... | collective-permute-start | bytes 393224 | tf_op jit(solution)/shard_map/ppermute | solution.py:33
  112.6 18.1 %collective-permute-start.8 = (bf16[32,2048]{1,0:T(8,128)(2,1)S(1)}, bf16[32,2048]{1,0:T(8,128)(2,1)S(1)}, u32[]{:S(2)}, u32[]{:S(2)}) collective-permute-start(bf16[32,2048]{1,0:T(8,128)(2,1)S(1)} %get-tuple-element.35), channel_id=1, source_target_pairs={{0,129},{1,130},{2,131},{3,128},{128,257},{129,258},{130,259},{131... | collective-permute-start | bytes 393224 | tf_op jit(solution)/shard_map/ppermute | solution.py:33
  114.5 18.7 %collective-permute-start.7 = (bf16[32,2048]{1,0:T(8,128)(2,1)S(1)}, bf16[32,2048]{1,0:T(8,128)(2,1)S(1)}, u32[]{:S(2)}, u32[]{:S(2)}) collective-permute-start(bf16[32,2048]{1,0:T(8,128)(2,1)S(1)} %get-tuple-element.36), channel_id=1, source_target_pairs={{0,128},{1,129},{2,130},{3,131},{128,256},{129,257},{130,258},{131... | collective-permute-start | bytes 393224 | tf_op jit(solution)/shard_map/ppermute | solution.py:33
